TPU v7x, 32 devices: a whole 2x2x4 slice. The times are simulated.
32 devices in a mesh: sky: 8 (over z, y), exp: 4 (over x, core).
Axes of the slice: x: 2, y: 2, z: 4, core: 2. Of those that a mesh axis runs over, the one named last changes fastest.
Arguments:
- sky_model: bfloat16 [2048, 1024], P('sky'), may hold values from -6 to 6
- exposure_data: bfloat16 [512, 128, 128], P(('sky', 'exp')), may hold values from -6 to 6
- pixel_mask: int32 [512, 128, 128], P(('sky', 'exp')), may hold values 0 or 1
- block_owner: int32 [512, 1], P(('sky', 'exp')), may hold values from 0 to 7; in each aligned block of 16 rows (0 to 15, 16 to 31, ...) at most 2 rows name the same one
- block_local: int32 [512], P(('sky', 'exp')), may hold values from 0 to 15
- psf_cell: int32 [512], P(('sky', 'exp')), may hold values from 0 to 15
- psf_table: bfloat16 [64, 1681], P('exp'), may hold values from -0.15625 to 0.15625
Outputs:
- model_grad: float32 [2048, 1024], P('sky', 'exp')
- residual: bfloat16 [512, 128, 128], P(('sky', 'exp'))
Inputs may be any that keep to these rules, and one draw needn't show every extreme that they name: `block_owner`: among the pieces of one device no sky index is named more than 2 times.
All inputs are finite; a program needn't handle non-finite values. No bound on the sum of `pixel_mask` on one device may be relied on, other than what follows from the above.
Results may differ from a plain program's by a relative error of at most 0.014.
Values may be sent and summed in bfloat16 or wider, within the bound.
A program may use at most 64 MiB of HBM per device.

v0:
```python
import jax
import jax.numpy as jnp
from jax import lax
from jax.sharding import PartitionSpec as P

B = 128
PSF = 41
HALO = 20
CAP = 2


def from_behind(x, axis, by):
    devices = lax.axis_size(axis)
    pairs = [(i, i + by) for i in range(devices) if 0 <= i + by < devices]
    return lax.ppermute(x, axis, pairs)


def banded_table(out_cols):
    width = out_cols + PSF - 1
    tap_index = lax.broadcasted_iota(jnp.int32, (PSF, width, out_cols), 0)
    column = lax.broadcasted_iota(jnp.int32, (PSF, width, out_cols), 1)
    target = lax.broadcasted_iota(jnp.int32, (PSF, width, out_cols), 2)
    return (column - target == tap_index).astype(jnp.bfloat16)


def correlate(field, kernel, table, out_rows):
    out_cols = table.shape[2]
    width = field.shape[1]
    banded = jnp.einsum("ab,bcj->caj", kernel, table, preferred_element_type=jnp.float32).astype(
        jnp.bfloat16
    )
    spread = jnp.dot(
        field, banded.reshape(width, PSF * out_cols), preferred_element_type=jnp.float32
    )
    total = spread[0:out_rows, 0:out_cols]
    for offset in range(1, PSF):
        total = (
            total + spread[offset : offset + out_rows, offset * out_cols : (offset + 1) * out_cols]
        )
    return total


def fold_blocks(per_block, block_rows, per_row):
    extent = B + 2 * HALO
    margin = 2 * HALO
    grid = per_block.reshape(block_rows, per_row, extent, extent)
    col_main = grid[..., :B].transpose(0, 2, 1, 3).reshape(block_rows, extent, per_row * B)
    col_tail = jnp.pad(grid[..., B:], ((0, 0), (0, 0), (0, 0), (0, B - margin)))
    col_tail = col_tail.transpose(0, 2, 1, 3).reshape(block_rows, extent, per_row * B)
    width = per_row * B + margin
    columns = (
        jnp.pad(col_main, ((0, 0), (0, 0), (0, margin)))
        + jnp.pad(col_tail, ((0, 0), (0, 0), (B, 0)))[:, :, :width]
    )
    row_main = columns[:, :B].reshape(block_rows * B, width)
    row_tail = jnp.pad(columns[:, B:], ((0, 0), (0, B - margin), (0, 0))).reshape(
        block_rows * B, width
    )
    height = block_rows * B + margin
    return jnp.pad(row_main, ((0, margin), (0, 0))) + jnp.pad(row_tail, ((B, 0), (0, 0)))[:height]


def shards(sky_model, exposure_data, pixel_mask, block_owner, block_local, psf_cell, psf_table):
    sky_count = lax.axis_size("sky")
    extent = B + 2 * HALO
    stripe_rows = sky_model.shape[0]
    stripe_cols = sky_model.shape[1]
    per_row = stripe_cols // B
    block_rows = stripe_rows // B
    block_total = block_rows * per_row
    piece_count = exposure_data.shape[0]
    slot_total = sky_count * CAP
    owner_sky = block_owner[:, 0]
    earlier = lax.broadcasted_iota(jnp.int32, (piece_count, piece_count), 1) < lax.broadcasted_iota(
        jnp.int32, (piece_count, piece_count), 0
    )
    same_owner = owner_sky[:, None] == owner_sky[None, :]
    rank_within = jnp.sum((same_owner & earlier).astype(jnp.int32), axis=1)
    slot_index = owner_sky * CAP + rank_within
    requests = (
        jnp.full((slot_total,), -1, jnp.int32)
        .at[slot_index]
        .set(block_local)
        .reshape(sky_count, CAP)
    )
    cell_count = psf_table.shape[0]
    cell_onehot = (psf_cell[:, None] == lax.broadcasted_iota(jnp.int32, (1, cell_count), 1)).astype(
        jnp.bfloat16
    )
    kernels_flat = jnp.dot(cell_onehot, psf_table, preferred_element_type=jnp.float32).astype(
        jnp.bfloat16
    )
    forward_table = banded_table(B)
    adjoint_table = banded_table(extent)

    def per_piece(item):
        patch, kernel, observed, keep = item
        predicted = correlate(patch, kernel, forward_table, B)
        residual = (keep.astype(jnp.float32) * (predicted - observed.astype(jnp.float32))).astype(
            jnp.bfloat16
        )
        widened = jnp.pad(residual, 2 * HALO)
        adjoint = correlate(widened, kernel[::-1, ::-1], adjoint_table, extent)
        return (residual, adjoint)

    whole = lax.all_gather(sky_model, "sky", axis=0, tiled=True)
    padded = jnp.pad(whole, HALO)
    row_start = (owner_sky * block_rows + block_local // per_row) * B
    col_start = block_local % per_row * B

    def cut_patch(row_first, col_first):
        return lax.dynamic_slice(padded, (row_first, col_first), (extent, extent))

    patches = jax.vmap(cut_patch)(row_start, col_start)
    kernels = kernels_flat.reshape(piece_count, PSF, PSF)
    residuals, adjoints = lax.map(per_piece, (patches, kernels, exposure_data, pixel_mask))
    outgoing = jnp.zeros((slot_total, extent, extent), jnp.float32).at[slot_index].set(adjoints)
    outgoing = outgoing.reshape(sky_count, CAP, extent, extent)
    received, received_ids = (
        lax.all_to_all(
            outgoing.astype(jnp.bfloat16), "sky", split_axis=0, concat_axis=0, tiled=True
        ).astype(outgoing.dtype),
        lax.all_to_all(requests, "sky", split_axis=0, concat_axis=0, tiled=True),
    )
    contributions = received.reshape(slot_total, extent, extent)
    asked_ids = received_ids.reshape(slot_total)
    selector = (asked_ids[:, None] == lax.broadcasted_iota(jnp.int32, (1, block_total), 1)).astype(
        jnp.float32
    )
    per_block = jnp.einsum("nl,nuv->luv", selector, contributions, precision=lax.Precision.HIGHEST)
    canvas = fold_blocks(per_block, block_rows, per_row)
    core = canvas[:, HALO : HALO + stripe_cols]
    from_below = from_behind(core[:HALO].astype(jnp.bfloat16), "sky", -1).astype(jnp.float32)
    from_above = from_behind(core[stripe_rows + HALO :].astype(jnp.bfloat16), "sky", 1).astype(
        jnp.float32
    )
    middle = core[HALO : stripe_rows + HALO]
    folded = (
        middle
        + jnp.pad(from_above, ((0, stripe_rows - HALO), (0, 0)))
        + jnp.pad(from_below, ((stripe_rows - HALO, 0), (0, 0)))
    )
    gradient = lax.psum_scatter(
        folded.astype(jnp.bfloat16), "exp", scatter_dimension=1, tiled=True
    ).astype(jnp.float32)
    return (gradient, residuals)


def solution(mesh):
    in_specs = (
        P("sky", None),
        P(("sky", "exp"), None, None),
        P(("sky", "exp"), None, None),
        P(("sky", "exp"), None),
        P(("sky", "exp")),
        P(("sky", "exp")),
        P("exp", None),
    )
    out_specs = (P("sky", "exp"), P(("sky", "exp"), None, None))
    return jax.shard_map(shards, mesh=mesh, in_specs=in_specs, out_specs=out_specs, check_vma=False)
```

profile of v0, /device:TPU:1, one launch (start us, length us, event | category | flops | bytes accessed | tf_op | source)
XLA Modules:
  0.0 400.3 jit_solution(16732655549156671051)
XLA Ops:
  10.9 6.4 %all-to-all-start = ((s32[8,1,2]{2,1,0:T(1,128)}), s32[8,1,2]{2,1,0:T(1,128)S(1)}, u32[]{:S(2)}, u32[]{:S(2)}) async-start(s32[8,1,2]{2,1,0:T(1,128)} %bitcast.3), calls=%async_computation | async-start | bytes 8192 | tf_op jit(solution)/shard_map/all_to_all | solution.py:123
  19.1 65.4 %all-gather.2.cloned.1.call-done = bf16[2048,1024]{1,0:T(8,128)(2,1)} async-done(((bf16[256,1024]{1,0:T(8,128)(2,1)}), bf16[2048,1024]{1,0:T(8,128)(2,1)}) %all-gather.2.cloned.1.call-update) | async-done | bytes 4194320 | tf_op jit(solution)/shard_map/all_gather | solution.py:106
  84.5 8.2 %pad.49 = bf16[2088,1064]{1,0:T(8,128)(2,1)} pad(bf16[2048,1024]{1,0:T(8,128)(2,1)} %all-gather.2.cloned.1.call-done, bf16[]{:T(256)} %constant.72.clone.1), padding=20_20x20_20 | pad | bytes 8637570 | tf_op jit(solution)/shard_map/jit(_pad)/pad | solution.py:107
  92.7 57.0 %while.16 = (s32[]{:T(128)}, bf16[2088,1064]{1,0:T(8,128)(2,1)}, s32[16,2]{0,1:T(2,128)S(1)}, bf16[16,168,168]{2,1,0:T(8,128)(2,1)}, s32[]{:T(128)}) while((s32[]{:T(128)}, bf16[2088,1064]{1,0:T(8,128)(2,1)}, s32[16,2]{0,1:T(2,128)S(1)}, bf16[16,168,168]{2,1,0:T(8,128)(2,1)}, s32[]{:T(128)}) %tuple.53), condition=%wide.while_cond, body=%wide.while_body.sunk | while | flops 2 | bytes 173665 | solution.py:112
  93.3 2.9 bitcast_dynamic-update-slice_fusion.4
  96.9 2.9 bitcast_dynamic-update-slice_fusion.4
  100.5 2.9 bitcast_dynamic-update-slice_fusion.4
  104.0 2.9 bitcast_dynamic-update-slice_fusion.4
  107.6 2.9 bitcast_dynamic-update-slice_fusion.4
  111.1 2.9 bitcast_dynamic-update-slice_fusion.4
  114.7 2.9 bitcast_dynamic-update-slice_fusion.4
  118.3 2.9 bitcast_dynamic-update-slice_fusion.4
  121.8 2.9 bitcast_dynamic-update-slice_fusion.4
  125.4 2.9 bitcast_dynamic-update-slice_fusion.4
  128.9 2.9 bitcast_dynamic-update-slice_fusion.4
  132.5 2.9 bitcast_dynamic-update-slice_fusion.4
  136.0 2.9 bitcast_dynamic-update-slice_fusion.4
  139.6 2.9 bitcast_dynamic-update-slice_fusion.4
  143.2 2.9 bitcast_dynamic-update-slice_fusion.4
  146.7 2.9 bitcast_dynamic-update-slice_fusion.4
  149.8 157.8 %while.17 = (s32[]{:T(128)}, bf16[16,128,128]{2,1,0:T(8,128)(2,1)}, f32[16,168,168]{2,1,0:T(8,128)S(1)}, s32[16,128,128]{2,1,0:T(8,128)}, bf16[16,168,168]{2,1,0...) while((s32[]{:T(128)}, bf16[16,128,128]{2,1,0:T(8,128)(2,1)}, ...), condition=%wide.region_3.4_spmd.clone, body=%wide.region_2.3_spmd.clone.sunk | while | flops 1093145856 | bytes 34470920 | solution.py:116
  157.7 1.9 fusion.82
  167.6 1.9 fusion.82
  197.2 1.9 fusion.82
  216.9 1.9 fusion.82
  309.3 3.1 scatter_fusion
  312.6 2.2 copy.21
  314.8 4.0 all-to-all-start.1
  320.0 29.9 %all-to-all-done.1 = bf16[8,2,168,168]{3,1,2,0:T(2,128)(2,1)S(1)} async-done(((bf16[8,2,168,168]{3,1,2,0:T(2,128)(2,1)}), bf16[8,2,168,168]{3,1,2,0:T(2,128)(2,1)S(1)}, u32[]{:S(2)}, u32[]{:S(2)}) %all-to-all-start.1) | async-done | bytes 903200 | tf_op jit(solution)/shard_map/all_to_all | solution.py:120
  359.0 4.1 %collective-permute-start = (bf16[20,1024]{1,0:T(8,128)(2,1)S(1)}, bf16[20,1024]{1,0:T(8,128)(2,1)S(1)}, u32[]{:S(2)}, u32[]{:S(2)}) collective-permute-start(bf16[20,1024]{1,0:T(8,128)(2,1)S(1)} %get-tuple-element.171), channel_id=1, source_target_pairs={{0,4},{4,8},{8,12},{12,16},{16,20},{20,24},{24,28},{1,5},{5,9},{9,... | collective-permute-start | bytes 122888 | tf_op jit(solution)/shard_map/ppermute | solution.py:15
  364.4 3.5 collective-permute-done.1
  369.1 22.7 %reduce-scatter.2.cloned.1.call-done = bf16[256,256]{1,0:T(8,128)(2,1)} async-done(((bf16[256,1024]{1,0:T(8,128)(2,1)}), bf16[256,256]{1,0:T(8,128)(2,1)}) %reduce-scatter.2.cloned.1.call-update) | async-done | bytes 131088 | tf_op jit(solution)/shard_map/reduce_scatter | solution.py:143
  (216 shorter events, 181.7 us)
Async XLA Ops:
  7.2 10.2 %copy-start = (bf16[16,1681]{1,0:T(8,128)(2,1)S(1)}, bf16[16,1681]{1,0:T(8,128)(2,1)}, u32[]{:S(2)}) copy-start(bf16[16,1681]{1,0:T(8,128)(2,1)} %param.15) | copy-start | bytes 161380
  7.2 77.3 %all-gather.2.cloned.1.call-start = ((), (), s32[]{:S(2)}) async-start(), calls=%async_computation.3 | async-start | bytes 4718592 | tf_op jit(solution)/shard_map/all_gather | solution.py:106
  10.9 303.8 %all-to-all-start = ((s32[8,1,2]{2,1,0:T(1,128)}), s32[8,1,2]{2,1,0:T(1,128)S(1)}, u32[]{:S(2)}, u32[]{:S(2)}) async-start(s32[8,1,2]{2,1,0:T(1,128)} %bitcast.3), calls=%async_computation | async-start | bytes 8192 | tf_op jit(solution)/shard_map/all_to_all | solution.py:123
  307.6 1.5 copy-start.1
  314.8 35.1 %all-to-all-start.1 = ((bf16[8,2,168,168]{3,1,2,0:T(2,128)(2,1)}), bf16[8,2,168,168]{3,1,2,0:T(2,128)(2,1)S(1)}, u32[]{:S(2)}, u32[]{:S(2)}) async-start(bf16[8,2,168,168]{3,1,2,0:T(2,128)(2,1)} %copy.21), calls=%async_computation.1 | async-start | bytes 2752512 | tf_op jit(solution)/shard_map/all_to_all | solution.py:120
  318.7 73.1 %reduce-scatter.2.cloned.1.call-start = ((), (), s32[]{:S(2)}) async-start(), calls=%async_computation.4 | async-start | bytes 655360 | tf_op jit(solution)/shard_map/reduce_scatter | solution.py:143
  359.0 5.4 %collective-permute-start = (bf16[20,1024]{1,0:T(8,128)(2,1)S(1)}, bf16[20,1024]{1,0:T(8,128)(2,1)S(1)}, u32[]{:S(2)}, u32[]{:S(2)}) collective-permute-start(bf16[20,1024]{1,0:T(8,128)(2,1)S(1)} %get-tuple-element.171), channel_id=1, source_target_pairs={{0,4},{4,8},{8,12},{12,16},{16,20},{20,24},{24,28},{1,5},{5,9},{9,... | collective-permute-start | bytes 122888 | tf_op jit(solution)/shard_map/ppermute | solution.py:15
  363.1 4.8 %collective-permute-start.1 = (bf16[20,1024]{1,0:T(8,128)(2,1)S(1)}, bf16[20,1024]{1,0:T(8,128)(2,1)S(1)}, u32[]{:S(2)}, u32[]{:S(2)}) collective-permute-start(bf16[20,1024]{1,0:T(8,128)(2,1)S(1)} %get-tuple-element.172), channel_id=1, source_target_pairs={{4,0},{8,4},{12,8},{16,12},{20,16},{24,20},{28,24},{5,1},{9,5},{13... | collective-permute-start | bytes 122888 | tf_op jit(solution)/shard_map/ppermute | solution.py:15
Sparse Core Ops, SparseCore 0:
  10.1 74.3 all-gather.1
  369.2 22.5 reduce-scatter.1
where the time goes:
time: 403 us; the launch traced here: 400 us
  waiting for transfers between devices  122 us (30%)
  local copies, waits for them, and re-layouts  103 us (26%)
  matrix products  77.6 us (19%)
  other arithmetic  66.5 us (17%)
  starting transfers between devices  15.8 us (4%)
  between operations  14.2 us (4%)
    all_gather x1, waiting for transfers between devices, shards(): whole = lax.all_gather(sky_model, 'sky', axis=0, tiled=True)  65.4 us
    dynamic_update_slice x32, other arithmetic, shards(): lax.map(per_piece, (patches, kernels, exposure_data, pixel_mask))  59 us
    gather x48, local copies, waits for them, and re-layouts  56.9 us
    dot_general x32, matrix products, correlate(): jnp.dot(field, banded.reshape(width, PSF * out_cols), preferred_element_t...  45.9 us
    dot_general x32, matrix products, correlate(): jnp.einsum('ab,bcj->caj', kernel, table, preferred_element_type=jnp.float32)  30.2 us
    all_to_all x1, waiting for transfers between devices, shards(): lax.all_to_all(outgoing.astype(jnp.bfloat16), 'sky', split_axis=0, concat...  29.9 us
    reduce_scatter x1, waiting for transfers between devices, shards(): lax.psum_scatter(folded.astype(jnp.bfloat16), 'exp', scatter_dimension=1,...  22.7 us
    convert_element_type x16, local copies, waits for them, and re-layouts, correlate(): jnp.einsum('ab,bcj->caj', kernel, table, preferred_element_type=jnp.float32)  20.1 us
  transfers between devices with their start and end apart: 6, of which 4 were waited for; matrix products, arithmetic and copies ran while one was open for 58% of the time, Pallas kernels for 0%

commit v1 on v0

v1 whole, which is shorter than its diff:
```python
import functools

import jax
import jax.numpy as jnp
from jax import lax
from jax.experimental import pallas as pl
from jax.experimental.pallas import tpu as pltpu
from jax.sharding import PartitionSpec as P

B = 128
PSF = 41
HALO = 20
CAP = 2
EXT = B + 2 * HALO
TAPS = 48
ROWPAD = 32
COLPAD = 128
AROWS = 176


def from_behind(x, axis, by):
    devices = lax.axis_size(axis)
    pairs = [(i, i + by) for i in range(devices) if 0 <= i + by < devices]
    return lax.ppermute(x, axis, pairs)


def fold_blocks(per_block, block_rows, per_row):
    extent = B + 2 * HALO
    margin = 2 * HALO
    grid = per_block.reshape(block_rows, per_row, extent, extent)
    col_main = grid[..., :B].transpose(0, 2, 1, 3).reshape(block_rows, extent, per_row * B)
    col_tail = jnp.pad(grid[..., B:], ((0, 0), (0, 0), (0, 0), (0, B - margin)))
    col_tail = col_tail.transpose(0, 2, 1, 3).reshape(block_rows, extent, per_row * B)
    width = per_row * B + margin
    columns = (
        jnp.pad(col_main, ((0, 0), (0, 0), (0, margin)))
        + jnp.pad(col_tail, ((0, 0), (0, 0), (B, 0)))[:, :, :width]
    )
    row_main = columns[:, :B].reshape(block_rows * B, width)
    row_tail = jnp.pad(columns[:, B:], ((0, 0), (0, B - margin), (0, 0))).reshape(
        block_rows * B, width
    )
    height = block_rows * B + margin
    return jnp.pad(row_main, ((0, margin), (0, 0))) + jnp.pad(row_tail, ((B, 0), (0, 0)))[:height]


def piece_kernel(row_ref, col_ref, cell_ref, slot_ref, whole, base, observed, keep,
                 residual_out, adjoint_out, tt, patch, rbuf):
    piece = pl.program_id(0)

    @pl.when(piece == 0)
    def _():
        tt[...] = jnp.zeros_like(tt)
        rbuf[...] = jnp.zeros_like(rbuf)

    lane = lax.broadcasted_iota(jnp.int32, (PSF, 16, 128), 2)
    taps = base[0].astype(jnp.float32)
    for step in range(B // 16):
        first = 16 * step
        turned = pltpu.roll(taps, first, 2) if first else taps
        over = first + 56 - 128
        if over > 0:
            low = jnp.where(lane >= first, turned, 0.0)
            high = jnp.where(lane < over, turned, 0.0)
            tt[0:PSF, first : first + 16, 128:256] = high.astype(jnp.bfloat16)
        else:
            low = turned
        tt[0:PSF, first : first + 16, 0:128] = low.astype(jnp.bfloat16)

    row0 = pl.multiple_of(row_ref[piece], 128)
    col0 = pl.multiple_of(col_ref[piece], 128)
    window = whole[pl.ds(row0, 192), pl.ds(col0, 384)].astype(jnp.float32)
    shifted = window[ROWPAD - HALO : ROWPAD - HALO + AROWS]
    shifted = pltpu.roll(shifted, 384 - (COLPAD - HALO), 1)[:, 0:256]
    patch[...] = shifted.astype(jnp.bfloat16)

    total = None
    for s in range(14, -1, -2):
        acc = None
        for q in range(3):
            a = 16 * q + s
            if a >= PSF:
                continue
            band = tt[a : a + 2].reshape(256, 256)
            term = lax.dot_general(patch[16 * q : 16 * q + 144, :], band,
                                   (((1,), (1,)), ((), ())), preferred_element_type=jnp.float32)
            acc = term if acc is None else acc + term
        if total is None:
            total = acc[:, 128:256]
        else:
            total = pltpu.roll(total, 143, 0) + acc[:, 128:256]
        total = pltpu.roll(total, 143, 0) + acc[:, 0:128]
    predicted = total[0:B]
    residual = (keep[0].astype(jnp.float32) * (predicted - observed[0].astype(jnp.float32)))
    residual = residual.astype(jnp.bfloat16)
    residual_out[0] = residual
    wide = jnp.concatenate([residual.astype(jnp.float32), jnp.zeros((16, B), jnp.float32)], 0)
    rbuf[32 : 32 + B, 0:128] = residual
    rbuf[32 : 32 + B + 16, 128:256] = pltpu.roll(wide, 1, 0).astype(jnp.bfloat16)

    back = None
    for s in range(14, -1, -2):
        acc = None
        for q in range(3):
            a = 16 * q + s
            if a >= PSF:
                continue
            band = tt[a : a + 2].reshape(256, 256)
            term = jnp.dot(rbuf[32 - 16 * q : 32 - 16 * q + AROWS, :], band,
                           preferred_element_type=jnp.float32)
            acc = term if acc is None else acc + term
        back = acc if back is None else pltpu.roll(back, 2, 0) + acc
    adjoint_out[0] = back.astype(jnp.bfloat16)


def run_pieces(rows, cols, cells, slots, whole, base, observed, keep, slot_total):
    count = observed.shape[0]
    flops = count * 21 * 2 * 256 * 256 * (144 + AROWS)
    return pl.pallas_call(
        piece_kernel,
        grid_spec=pltpu.PrefetchScalarGridSpec(
            num_scalar_prefetch=4,
            grid=(count,),
            in_specs=[
                pl.BlockSpec(whole.shape, lambda p, r, c, k, s: (0, 0)),
                pl.BlockSpec((1, PSF, 16, 128), lambda p, r, c, k, s: (k[p], 0, 0, 0)),
                pl.BlockSpec((1, B, B), lambda p, r, c, k, s: (p, 0, 0)),
                pl.BlockSpec((1, B, B), lambda p, r, c, k, s: (p, 0, 0)),
            ],
            out_specs=[
                pl.BlockSpec((1, B, B), lambda p, r, c, k, s: (p, 0, 0)),
                pl.BlockSpec((1, AROWS, 256), lambda p, r, c, k, s: (s[p], 0, 0)),
            ],
            scratch_shapes=[
                pltpu.VMEM((TAPS, B, 256), jnp.bfloat16),
                pltpu.VMEM((AROWS, 256), jnp.bfloat16),
                pltpu.VMEM((32 + AROWS, 256), jnp.bfloat16),
            ],
        ),
        out_shape=[
            jax.ShapeDtypeStruct((count, B, B), jnp.bfloat16),
            jax.ShapeDtypeStruct((slot_total, AROWS, 256), jnp.bfloat16),
        ],
        compiler_params=pltpu.CompilerParams(vmem_limit_bytes=56 * 2**20),
        cost_estimate=pl.CostEstimate(flops=flops, bytes_accessed=16 * 2**20, transcendentals=0),
        name="pieces",
    )(rows, cols, cells, slots, whole, base, observed, keep)


def shards(sky_model, exposure_data, pixel_mask, block_owner, block_local, psf_cell, psf_table):
    sky_count = lax.axis_size("sky")
    extent = EXT
    stripe_rows = sky_model.shape[0]
    stripe_cols = sky_model.shape[1]
    per_row = stripe_cols // B
    block_rows = stripe_rows // B
    block_total = block_rows * per_row
    piece_count = exposure_data.shape[0]
    slot_total = sky_count * CAP
    owner_sky = block_owner[:, 0]
    earlier = lax.broadcasted_iota(jnp.int32, (piece_count, piece_count), 1) < lax.broadcasted_iota(
        jnp.int32, (piece_count, piece_count), 0
    )
    same_owner = owner_sky[:, None] == owner_sky[None, :]
    rank_within = jnp.sum((same_owner & earlier).astype(jnp.int32), axis=1)
    slot_index = owner_sky * CAP + rank_within
    requests_flat = jnp.full((slot_total,), -1, jnp.int32).at[slot_index].set(block_local)
    requests = requests_flat.reshape(sky_count, CAP)
    cell_count = psf_table.shape[0]
    kernels = psf_table.reshape(cell_count, PSF, PSF)
    base = jnp.stack(
        [jnp.pad(kernels, ((0, 0), (0, 0), (j, 128 - PSF - j))) for j in range(16)], axis=2
    )

    whole = lax.all_gather(sky_model, "sky", axis=0, tiled=True)
    padded = jnp.pad(whole, ((ROWPAD, ROWPAD), (COLPAD, COLPAD)))
    row_start = (owner_sky * block_rows + block_local // per_row) * B
    col_start = block_local % per_row * B
    residuals, adjoints = run_pieces(
        row_start, col_start, psf_cell, slot_index, padded, base, exposure_data, pixel_mask, slot_total
    )
    outgoing = jnp.where((requests_flat >= 0)[:, None, None], adjoints, 0)[:, :extent, :extent]
    outgoing = outgoing.reshape(sky_count, CAP, extent, extent)
    received, received_ids = (
        lax.all_to_all(outgoing, "sky", split_axis=0, concat_axis=0, tiled=True).astype(jnp.float32),
        lax.all_to_all(requests, "sky", split_axis=0, concat_axis=0, tiled=True),
    )
    contributions = received.reshape(slot_total, extent, extent)
    asked_ids = received_ids.reshape(slot_total)
    selector = (asked_ids[:, None] == lax.broadcasted_iota(jnp.int32, (1, block_total), 1)).astype(
        jnp.float32
    )
    per_block = jnp.einsum("nl,nuv->luv", selector, contributions, precision=lax.Precision.HIGHEST)
    canvas = fold_blocks(per_block, block_rows, per_row)
    core = canvas[:, HALO : HALO + stripe_cols]
    from_below = from_behind(core[:HALO].astype(jnp.bfloat16), "sky", -1).astype(jnp.float32)
    from_above = from_behind(core[stripe_rows + HALO :].astype(jnp.bfloat16), "sky", 1).astype(
        jnp.float32
    )
    middle = core[HALO : stripe_rows + HALO]
    folded = (
        middle
        + jnp.pad(from_above, ((0, stripe_rows - HALO), (0, 0)))
        + jnp.pad(from_below, ((stripe_rows - HALO, 0), (0, 0)))
    )
    gradient = lax.psum_scatter(
        folded.astype(jnp.bfloat16), "exp", scatter_dimension=1, tiled=True
    ).astype(jnp.float32)
    return (gradient, residuals)


def solution(mesh):
    in_specs = (
        P("sky", None),
        P(("sky", "exp"), None, None),
        P(("sky", "exp"), None, None),
        P(("sky", "exp"), None),
        P(("sky", "exp")),
        P(("sky", "exp")),
        P("exp", None),
    )
    out_specs = (P("sky", "exp"), P(("sky", "exp"), None, None))
    return jax.shard_map(shards, mesh=mesh, in_specs=in_specs, out_specs=out_specs, check_vma=False)
```

time: 403 us -> 209 us (0.52)
  matrix products: 77.6 us -> 0.57 us
  local copies, waits for them, and re-layouts: 103 us -> 37 us
  other arithmetic: 66.5 us -> 9.75 us
  Pallas kernels: 0 us -> 32.1 us
  waiting for transfers between devices: 122 us -> 97.6 us
    dot_general x65 -> x0, matrix products: 77 us -> none  [the longest x32 45.9 us: correlate(): jnp.dot(field, banded.reshape(width, PSF * out_cols), preferred_element_t...]
    dynamic_update_slice x32 -> x0, other arithmetic: 59 us -> none  [shards(): lax.map(per_piece, (patches, kernels, exposure_data, pixel_mask))]
    gather x48 -> x0, local copies, waits for them, and re-layouts: 56.9 us -> none
    pallas_call x0 -> x1, Pallas kernels: none -> 32.1 us  [run_pieces(): pl.pallas_call(piece_kernel, grid_spec=pltpu.PrefetchScalarGridSpec(num_s...]
    all_gather x1, waiting for transfers between devices: 65.4 us -> 40.9 us  [shards(): whole = lax.all_gather(sky_model, 'sky', axis=0, tiled=True)]
    another operation x2 -> x18, local copies, waits for them, and re-layouts: 0.36 us -> 24.6 us  [shards(): jnp.stack([jnp.pad(kernels, ((0, 0), (0, 0), (j, 128 - PSF - j))) for j i...]
    convert_element_type x17 -> x0, local copies, waits for them, and re-layouts: 22.3 us -> none  [the longest x16 20.1 us: correlate(): jnp.einsum('ab,bcj->caj', kernel, table, preferred_element_type=jnp.float32)]
  transfers between devices with their start and end apart: 6 -> 6, of which waited for: 4 -> 4; matrix products, arithmetic and copies ran while one was open for 58% -> 18% of each run, Pallas kernels for 0% -> 15%
where the time goes in v1:
time: 209 us; the launch traced here: 207 us
  waiting for transfers between devices  97.6 us (47%)
  local copies, waits for them, and re-layouts  37 us (18%)
  Pallas kernels  32.1 us (15%)
  starting transfers between devices  16 us (8%)
  between operations  14.3 us (7%)
  other arithmetic  9.75 us (5%)
    all_gather x1, waiting for transfers between devices, shards(): whole = lax.all_gather(sky_model, 'sky', axis=0, tiled=True)  40.9 us
    pallas_call x1, Pallas kernels, run_pieces(): pl.pallas_call(piece_kernel, grid_spec=pltpu.PrefetchScalarGridSpec(num_s...  32.1 us
    all_to_all x1, waiting for transfers between devices, shards(): lax.all_to_all(outgoing, 'sky', split_axis=0, concat_axis=0, tiled=True)  29.7 us
    another operation x18, local copies, waits for them, and re-layouts, shards(): jnp.stack([jnp.pad(kernels, ((0, 0), (0, 0), (j, 128 - PSF - j))) for j i...  24.6 us
    reduce_scatter x1, waiting for transfers between devices, shards(): lax.psum_scatter(folded.astype(jnp.bfloat16), 'exp', scatter_dimension=1,...  22.8 us
    all_to_all x1, starting transfers between devices, shards(): lax.all_to_all(requests, 'sky', split_axis=0, concat_axis=0, tiled=True)  6.38 us
    ppermute x2, starting transfers between devices, from_behind(): return lax.ppermute(x, axis, pairs)  5.41 us
    pad x1, local copies, waits for them, and re-layouts, shards(): padded = jnp.pad(whole, ((ROWPAD, ROWPAD), (COLPAD, COLPAD)))  4.92 us
  transfers between devices with their start and end apart: 6, of which 4 were waited for; matrix products, arithmetic and copies ran while one was open for 18% of the time, Pallas kernels for 15%

profile of v1, /device:TPU:1, one launch (start us, length us, event | category | flops | bytes accessed | tf_op | source)
XLA Modules:
  0.0 207.2 jit_solution(17407973265662547952)
XLA Ops:
  7.2 0.7 all-gather.2.cloned.1.call-update
  7.9 0.9 convert_reduce_fusion
  8.8 0.7 fusion.12
  9.5 0.8 scatter_custom_fusion
  10.2 0.7 all_to_all.9
  10.9 6.4 %all-to-all-start = ((s32[8,1,2]{2,1,0:T(1,128)}), s32[8,1,2]{2,1,0:T(1,128)S(1)}, u32[]{:S(2)}, u32[]{:S(2)}) async-start(s32[8,1,2]{2,1,0:T(1,128)} %bitcast.3), calls=%async_computation | async-start | bytes 8192 | tf_op jit(solution)/shard_map/all_to_all | solution.py:186
  17.3 1.1 reshape.53
  18.4 0.8 pad_bitcast_fusion.1
  21.9 1.0 copy.122
  22.9 1.0 copy.123
  23.9 1.0 copy.124
  24.9 1.0 copy.125
  25.9 1.0 copy.126
  26.9 1.0 copy.127
  27.9 15.2 %stack.67.base = bf16[16,41,16,128]{3,2,1,0:T(8,128)(2,1)} concatenate(bf16[16,41,1,128]{3,2,1,0:T(2,128)(2,1)S(1)} %copy.112, bf16[16,41,1,128]{3,2,1,0:T(2,128)(2,1)S(1)} %copy.113, bf16[16,41,1,128]{3,2,1,0:T(2,128)(2,1)S(1)} %copy.114, bf16[16,41,1,128]{3,2,1,0:T(2,128)(2,1)S(1)} %copy.115, bf16[16,41,1,128]{3,2,1,0:T(2,128)(2,1)S(1)} %copy.116, ...), dimensions={2} | concatenate | bytes 5373952 | tf_op jit(solution)/shard_map/stack | solution.py:171
  43.6 40.9 %all-gather.2.cloned.1.call-done = bf16[2048,1024]{1,0:T(8,128)(2,1)} async-done(((bf16[256,1024]{1,0:T(8,128)(2,1)}), bf16[2048,1024]{1,0:T(8,128)(2,1)}) %all-gather.2.cloned.1.call-update) | async-done | bytes 4194320 | tf_op jit(solution)/shard_map/all_gather | solution.py:175
  84.5 4.9 %pad.106.whole = bf16[2112,1280]{1,0:T(8,128)(2,1)} pad(bf16[2048,1024]{1,0:T(8,128)(2,1)} %all-gather.2.cloned.1.call-done, bf16[]{:T(256)} %constant.41.clone.1), padding=32_32x128_128 | pad | bytes 9601026 | tf_op jit(solution)/shard_map/jit(_pad)/pad | solution.py:176
  89.4 32.1 %pieces.1 = (bf16[16,128,128]{2,1,0:T(8,128)(2,1)}, bf16[16,176,256]{2,1,0:T(8,128)(2,1)}) custom-call(s32[16]{0:T(128)} %get-tuple-element.27.row_ref, s32[16]{0:T(128)} %get-tuple-element.28.col_ref, s32[16]{0:T(128)} %cell_ref.1, s32[16]{0:T(128)} %get-tuple-element.26.slot_ref, bf16[2112,1280]{1,0:T(8,128)(2,1)} %pad.106.whole, ...), custom_call_target="tpu_custom_call" | custom-call | flops 14092861440 | bytes 16777216 | tf_op jit(solution)/shard_map/pieces/pallas_call | solution.py:119
  121.4 2.6 %slice_select_fusion = bf16[16,168,168]{2,1,0:T(8,128)(2,1)} fusion(bf16[16,176,256]{2,1,0:T(8,128)(2,1)} %get-tuple-element.4, pred[16]{0:T(512)(128)(4,1)S(1)} %broadcast_compare_fusion), kind=kLoop, calls=%fused_computation.4 | loop fusion | flops 451584 | bytes 1806352 | tf_op jit(solution)/shard_map/jit(_where)/select_n | solution.py:182
  124.1 3.9 %all-to-all-start.1 = ((bf16[8,2,168,168]{3,2,1,0:T(8,128)(2,1)}), bf16[8,2,168,168]{3,2,1,0:T(8,128)(2,1)S(1)}, u32[]{:S(2)}, u32[]{:S(2)}) async-start(bf16[8,2,168,168]{3,2,1,0:T(8,128)(2,1)} %bitcast.22), calls=%async_computation.1 | async-start | bytes 2752512 | tf_op jit(solution)/shard_map/all_to_all | solution.py:185
  128.7 0.7 reduce.3
  129.5 29.7 %all-to-all-done.1 = bf16[8,2,168,168]{3,2,1,0:T(8,128)(2,1)S(1)} async-done(((bf16[8,2,168,168]{3,2,1,0:T(8,128)(2,1)}), bf16[8,2,168,168]{3,2,1,0:T(8,128)(2,1)S(1)}, u32[]{:S(2)}, u32[]{:S(2)}) %all-to-all-start.1) | async-done | bytes 903200 | tf_op jit(solution)/shard_map/all_to_all | solution.py:185
  159.9 1.2 pad_bitcast_fusion
  161.1 1.5 reshape.57
  162.6 1.3 reshape.56
  163.9 1.5 slice_add_fusion
  165.9 4.1 %collective-permute-start = (bf16[20,1024]{1,0:T(8,128)(2,1)S(1)}, bf16[20,1024]{1,0:T(8,128)(2,1)S(1)}, u32[]{:S(2)}, u32[]{:S(2)}) collective-permute-start(bf16[20,1024]{1,0:T(8,128)(2,1)S(1)} %get-tuple-element.8), channel_id=1, source_target_pairs={{0,4},{4,8},{8,12},{12,16},{16,20},{20,24},{24,28},{1,5},{5,9},{9,... | collective-permute-start | bytes 122888 | tf_op jit(solution)/shard_map/ppermute | solution.py:24
  170.1 1.3 collective-permute-start.1
  171.4 3.5 %collective-permute-done.1 = bf16[20,1024]{1,0:T(8,128)(2,1)S(1)} collective-permute-done((bf16[20,1024]{1,0:T(8,128)(2,1)S(1)}, bf16[20,1024]{1,0:T(8,128)(2,1)S(1)}, u32[]{:S(2)}, u32[]{:S(2)}) %collective-permute-start.1) | collective-permute-done | bytes 40992 | tf_op jit(solution)/shard_map/ppermute | solution.py:24
  174.9 1.1 fusion.5
  176.0 22.8 %reduce-scatter.2.cloned.1.call-done = bf16[256,256]{1,0:T(8,128)(2,1)} async-done(((bf16[256,1024]{1,0:T(8,128)(2,1)}), bf16[256,256]{1,0:T(8,128)(2,1)}) %reduce-scatter.2.cloned.1.call-update) | async-done | bytes 131088 | tf_op jit(solution)/shard_map/reduce_scatter | solution.py:206
  198.8 1.6 convert_element_type.60
  (32 shorter events, 5.2 us)
Async XLA Ops:
  7.2 77.3 %all-gather.2.cloned.1.call-start = ((), (), s32[]{:S(2)}) async-start(), calls=%async_computation.3 | async-start | bytes 4718592 | tf_op jit(solution)/shard_map/all_gather | solution.py:175
  10.9 113.1 %all-to-all-start = ((s32[8,1,2]{2,1,0:T(1,128)}), s32[8,1,2]{2,1,0:T(1,128)S(1)}, u32[]{:S(2)}, u32[]{:S(2)}) async-start(s32[8,1,2]{2,1,0:T(1,128)} %bitcast.3), calls=%async_computation | async-start | bytes 8192 | tf_op jit(solution)/shard_map/all_to_all | solution.py:186
  27.9 15.2 %copy-start = (s32[16,1]{0,1:T(1,128)S(1)}, s32[16,1]{0,1:T(1,128)}, u32[]{:S(2)}) copy-start(s32[16,1]{0,1:T(1,128)} %param.10) | copy-start | bytes 196
  27.9 15.2 %copy-start.1 = (s32[16]{0:T(128)S(1)}, s32[16]{0:T(128)}, u32[]{:S(2)}) copy-start(s32[16]{0:T(128)} %param.11) | copy-start | bytes 196
  124.1 35.1 %all-to-all-start.1 = ((bf16[8,2,168,168]{3,2,1,0:T(8,128)(2,1)}), bf16[8,2,168,168]{3,2,1,0:T(8,128)(2,1)S(1)}, u32[]{:S(2)}, u32[]{:S(2)}) async-start(bf16[8,2,168,168]{3,2,1,0:T(8,128)(2,1)} %bitcast.22), calls=%async_computation.1 | async-start | bytes 2752512 | tf_op jit(solution)/shard_map/all_to_all | solution.py:185
  128.0 70.8 %reduce-scatter.2.cloned.1.call-start = ((), (), s32[]{:S(2)}) async-start(), calls=%async_computation.4 | async-start | bytes 655360 | tf_op jit(solution)/shard_map/reduce_scatter | solution.py:206
  165.9 5.4 %collective-permute-start = (bf16[20,1024]{1,0:T(8,128)(2,1)S(1)}, bf16[20,1024]{1,0:T(8,128)(2,1)S(1)}, u32[]{:S(2)}, u32[]{:S(2)}) collective-permute-start(bf16[20,1024]{1,0:T(8,128)(2,1)S(1)} %get-tuple-element.8), channel_id=1, source_target_pairs={{0,4},{4,8},{8,12},{12,16},{16,20},{20,24},{24,28},{1,5},{5,9},{9,... | collective-permute-start | bytes 122888 | tf_op jit(solution)/shard_map/ppermute | solution.py:24
  170.1 4.8 %collective-permute-start.1 = (bf16[20,1024]{1,0:T(8,128)(2,1)S(1)}, bf16[20,1024]{1,0:T(8,128)(2,1)S(1)}, u32[]{:S(2)}, u32[]{:S(2)}) collective-permute-start(bf16[20,1024]{1,0:T(8,128)(2,1)S(1)} %get-tuple-element.9), channel_id=1, source_target_pairs={{4,0},{8,4},{12,8},{16,12},{20,16},{24,20},{28,24},{5,1},{9,5},{13... | collective-permute-start | bytes 122888 | tf_op jit(solution)/shard_map/ppermute | solution.py:24
Sparse Core Ops, SparseCore 0:
  10.1 74.2 all-gather.1
  176.1 22.6 reduce-scatter.1

commit v2 on v1

v2 whole, which is shorter than its diff:
```python
import functools

import jax
import jax.numpy as jnp
from jax import lax
from jax.experimental import pallas as pl
from jax.experimental.pallas import tpu as pltpu
from jax.sharding import PartitionSpec as P

B = 128
PSF = 41
HALO = 20
CAP = 2
EXT = B + 2 * HALO
TAPS = 48
ROWPAD = 32
COLPAD = 128
AROWS = 176


MESH = pl.DeviceIdType.MESH
PACKED = 224
FOLD = 56
RIM = 32


def ring_place(sky, count):
    odd = sky % 2
    return (sky // 2) * (1 - odd) + (count - 1 - sky // 2) * odd


def ring_sky(place, count):
    late = place // (count // 2)
    return 2 * place * (1 - late) + (2 * (count - 1 - place) + 1) * late


def gather_kernel(count, cuts, stripe, whole, zero, ring_send, ring_recv, pair_send, pair_recv, local_sem):
    sky = lax.axis_index("sky")
    own = lax.axis_index("exp")
    core = own % 2
    pair = own + 1 - 2 * core
    place = ring_place(sky, count)
    ahead = ring_sky((place + 1) % count, count)
    behind = ring_sky((place + count - 1) % count, count)
    rows, cols = stripe.shape
    part = rows // (4 * cuts)

    barrier = pltpu.get_barrier_semaphore()
    for target in ((ahead, own), (behind, own), (sky, pair)):
        pl.semaphore_signal(barrier, inc=1, device_id=target, device_id_type=MESH)
    pl.semaphore_wait(barrier, 3)

    def inner(way, cut):
        return core * (rows // 2) + way * (rows // 4) + cut * part

    def spot(origin, way, cut):
        first = pl.multiple_of(ROWPAD + origin * rows + inner(way, cut), 16)
        return whole.at[pl.ds(first, part), pl.ds(COLPAD, cols)]

    def ring_copy(step, way, cut):
        sign = 1 - 2 * way
        origin = ring_sky((place + count - sign * step) % count, count)
        if step == 0:
            block = stripe.at[pl.ds(pl.multiple_of(inner(way, cut), 16), part), :]
        else:
            block = spot(origin, way, cut)
        return pltpu.make_async_remote_copy(
            src_ref=block, dst_ref=spot(origin, way, cut),
            send_sem=ring_send.at[step, way, cut], recv_sem=ring_recv.at[step, way, cut],
            device_id=((behind if way else ahead), own), device_id_type=MESH)

    def pair_copy(step, way, cut):
        sign = 1 - 2 * way
        origin = ring_sky((place + count - sign * step) % count, count)
        return pltpu.make_async_remote_copy(
            src_ref=spot(origin, way, cut), dst_ref=spot(origin, way, cut),
            send_sem=pair_send.at[step - 1, way, cut], recv_sem=pair_recv.at[step - 1, way, cut],
            device_id=(sky, pair), device_id_type=MESH)

    sends, pairs = {}, []
    for cut in range(cuts):
        for way in range(2):
            sends[0, way, cut] = ring_copy(0, way, cut)
            sends[0, way, cut].start()

    zero[...] = jnp.zeros_like(zero)
    total = whole.shape[0]
    fills = []
    mine = pl.multiple_of(ROWPAD + sky * rows, 16)
    fills.append(pltpu.make_async_copy(stripe, whole.at[pl.ds(mine, rows), pl.ds(COLPAD, cols)], local_sem.at[0]))
    for side in range(2):
        fills.append(pltpu.make_async_copy(
            zero, whole.at[:, pl.ds(side * (COLPAD + cols), COLPAD)], local_sem.at[1 + side]))
    for side in range(2):
        for block in range(cols // COLPAD):
            fills.append(pltpu.make_async_copy(
                zero.at[pl.ds(0, ROWPAD), :],
                whole.at[pl.ds(side * (total - ROWPAD), ROWPAD), pl.ds(COLPAD * (1 + block), COLPAD)],
                local_sem.at[3 + side * (cols // COLPAD) + block]))
    for fill in fills:
        fill.start()

    for step in range(1, count):
        for cut in range(cuts):
            for way in range(2):
                sends[step - 1, way, cut].wait_recv()
                if step < count - 1:
                    sends[step, way, cut] = ring_copy(step, way, cut)
                    sends[step, way, cut].start()
                extra = pair_copy(step, way, cut)
                extra.start()
                pairs.append((step, way, cut, extra))
    for copy in sends.values():
        copy.wait_send()
    for step, way, cut, extra in pairs:
        extra.wait_send()
        extra.wait_recv()
    for fill in fills:
        fill.wait()


def gather_model(stripe):
    count = lax.axis_size("sky")
    rows, cols = stripe.shape
    cuts = 2
    shape = (count * rows + 2 * ROWPAD, cols + 2 * COLPAD)
    steps = (count - 1, 2, cuts)
    return pl.pallas_call(
        functools.partial(gather_kernel, count, cuts),
        out_shape=jax.ShapeDtypeStruct(shape, stripe.dtype),
        in_specs=[pl.BlockSpec(memory_space=pl.ANY)],
        out_specs=pl.BlockSpec(memory_space=pl.ANY),
        scratch_shapes=[
            pltpu.VMEM((shape[0], COLPAD), stripe.dtype),
            pltpu.SemaphoreType.DMA(steps),
            pltpu.SemaphoreType.DMA(steps),
            pltpu.SemaphoreType.DMA(steps),
            pltpu.SemaphoreType.DMA(steps),
            pltpu.SemaphoreType.DMA((3 + 2 * (cols // COLPAD),)),
        ],
        compiler_params=pltpu.CompilerParams(
            collective_id=0, has_side_effects=True, vmem_limit_bytes=32 * 2**20),
        name="gather_model",
    )(stripe)


def exchange_kernel(count, data, asked, got, got_asked, data_send, data_recv, id_send, id_recv, local_sem):
    sky = lax.axis_index("sky")
    own = lax.axis_index("exp")
    barrier = pltpu.get_barrier_semaphore()
    for turn in range(1, count):
        pl.semaphore_signal(barrier, inc=1, device_id=((sky + turn) % count, own), device_id_type=MESH)
    pl.semaphore_wait(barrier, count - 1)
    copies = []
    for turn in range(1, count):
        target = (sky + turn) % count
        for source, dest, send, recv in ((data, got, data_send, data_recv), (asked, got_asked, id_send, id_recv)):
            copy = pltpu.make_async_remote_copy(
                src_ref=source.at[target], dst_ref=dest.at[sky],
                send_sem=send.at[turn - 1], recv_sem=recv.at[turn - 1],
                device_id=(target, own), device_id_type=MESH)
            copy.start()
            copies.append(copy)
    for place, (source, dest) in enumerate(((data, got), (asked, got_asked))):
        copy = pltpu.make_async_copy(source.at[sky], dest.at[sky], local_sem.at[place])
        copy.start()
        copies.append(copy)
    for copy in copies:
        copy.wait()


def exchange(data, asked):
    count = lax.axis_size("sky")
    return pl.pallas_call(
        functools.partial(exchange_kernel, count),
        out_shape=[jax.ShapeDtypeStruct(x.shape, x.dtype) for x in (data, asked)],
        in_specs=[pl.BlockSpec(memory_space=pl.ANY)] * 2,
        out_specs=[pl.BlockSpec(memory_space=pl.ANY)] * 2,
        scratch_shapes=[pltpu.SemaphoreType.DMA((count - 1,))] * 4 + [pltpu.SemaphoreType.DMA((2,))],
        compiler_params=pltpu.CompilerParams(
            collective_id=1, has_side_effects=True, vmem_limit_bytes=32 * 2**20),
        name="exchange",
    )(data, asked)


def fold_kernel(stripe_rows, stripe_cols, exps, ids, parts, out, canvas):
    per_row = stripe_cols // B
    canvas[...] = jnp.zeros_like(canvas)
    lane = lax.broadcasted_iota(jnp.int32, (FOLD, B), 1)

    def add(slot, carry):
        block = ids[slot]

        @pl.when(block >= 0)
        def _():
            row0 = pl.multiple_of(block // per_row * B, B)
            col0 = pl.multiple_of(block % per_row * B, B)
            values = parts[slot].astype(jnp.float32)
            canvas[pl.ds(row0, EXT), pl.ds(col0, B)] += values[0:EXT]
            tails = values[EXT:PACKED]
            for third in range(3):
                turned = pltpu.roll(tails, B - 2 * HALO * third, 1) if third else tails
                turned = jnp.where(lane < 2 * HALO, turned, 0.0)
                first = pl.multiple_of(row0 + FOLD * third, 8)
                canvas[pl.ds(first, FOLD), pl.ds(pl.multiple_of(col0 + B, B), B)] += turned

        return carry

    lax.fori_loop(0, ids.shape[0], add, 0)
    width = stripe_cols + B
    middle = pltpu.roll(canvas[...], width - HALO, 1)[:, 0:stripe_cols]
    upper = jnp.concatenate([jnp.zeros((RIM - HALO, stripe_cols), jnp.float32), middle[0:HALO]], 0)
    lower = middle[stripe_rows + HALO : stripe_rows + HALO + RIM]
    rows = jnp.concatenate([middle[HALO : HALO + stripe_rows], upper, lower], 0).astype(out.dtype)
    share = stripe_cols // exps
    for e in range(exps):
        out[e] = rows[:, e * share : (e + 1) * share]


def fold(ids, parts, stripe_rows, stripe_cols, exps):
    shape = (exps, stripe_rows + 2 * RIM, stripe_cols // exps)
    return pl.pallas_call(
        functools.partial(fold_kernel, stripe_rows, stripe_cols, exps),
        grid_spec=pltpu.PrefetchScalarGridSpec(
            num_scalar_prefetch=1,
            grid=(1,),
            in_specs=[pl.BlockSpec(parts.shape, lambda i, ids: (0, 0, 0))],
            out_specs=pl.BlockSpec(shape, lambda i, ids: (0, 0, 0)),
            scratch_shapes=[pltpu.VMEM((stripe_rows + 56, stripe_cols + B), jnp.float32)],
        ),
        out_shape=jax.ShapeDtypeStruct(shape, jnp.bfloat16),
        compiler_params=pltpu.CompilerParams(vmem_limit_bytes=40 * 2**20),
        name="fold",
    )(ids, parts)


def reduce_kernel(skies, exps, parts, out, held, rims, rims_in, send, recv, rim_send, rim_recv):
    sky = lax.axis_index("sky")
    own = lax.axis_index("exp")
    above, below = (sky + skies - 1) % skies, (sky + 1) % skies
    rows = out.shape[0]
    barrier = pltpu.get_barrier_semaphore()
    targets = [(sky, (own + turn) % exps) for turn in range(1, exps)] + [(above, own), (below, own)]
    for target in targets:
        pl.semaphore_signal(barrier, inc=1, device_id=target, device_id_type=MESH)
    pl.semaphore_wait(barrier, len(targets))
    copies = []
    for turn in range(1, exps):
        target = (own + turn) % exps
        copy = pltpu.make_async_remote_copy(
            src_ref=parts.at[target], dst_ref=held.at[turn - 1],
            send_sem=send.at[turn - 1], recv_sem=recv.at[turn - 1],
            device_id=(sky, target), device_id_type=MESH)
        copy.start()
        copies.append(copy)
    for copy in copies:
        copy.wait_recv()

    def total(first, size):
        value = parts[own, first : first + size].astype(jnp.float32)
        for turn in range(1, exps):
            value = value + held[turn - 1, first : first + size].astype(jnp.float32)
        return value

    rims[0] = total(rows, RIM).astype(rims.dtype)
    rims[1] = total(rows + RIM, RIM).astype(rims.dtype)
    for side, target in enumerate((above, below)):
        copy = pltpu.make_async_remote_copy(
            src_ref=rims.at[side], dst_ref=rims_in.at[side],
            send_sem=rim_send.at[side], recv_sem=rim_recv.at[side],
            device_id=(target, own), device_id_type=MESH)
        copy.start()
        copies.append(copy)
    out[RIM : rows - RIM] = total(RIM, rows - 2 * RIM)
    top = total(0, RIM)
    bottom = total(rows - RIM, RIM)
    for copy in copies[-2:]:
        copy.wait_recv()
    has_above = jnp.full(top.shape, sky, jnp.int32) > 0
    has_below = jnp.full(top.shape, sky, jnp.int32) < skies - 1
    out[0:RIM] = top + jnp.where(has_above, rims_in[1].astype(jnp.float32), 0.0)
    out[rows - RIM : rows] = bottom + jnp.where(has_below, rims_in[0].astype(jnp.float32), 0.0)
    for copy in copies:
        copy.wait_send()


def reduce_parts(parts):
    skies, exps = lax.axis_size("sky"), lax.axis_size("exp")
    _, height, share = parts.shape
    rim = (2, RIM, share)
    return pl.pallas_call(
        functools.partial(reduce_kernel, skies, exps),
        out_shape=jax.ShapeDtypeStruct((height - 2 * RIM, share), jnp.float32),
        in_specs=[pl.BlockSpec(memory_space=pltpu.VMEM)],
        out_specs=pl.BlockSpec(memory_space=pltpu.VMEM),
        scratch_shapes=[
            pltpu.VMEM((exps - 1, height, share), parts.dtype),
            pltpu.VMEM(rim, parts.dtype),
            pltpu.VMEM(rim, parts.dtype),
            pltpu.SemaphoreType.DMA((exps - 1,)),
            pltpu.SemaphoreType.DMA((exps - 1,)),
            pltpu.SemaphoreType.DMA((2,)),
            pltpu.SemaphoreType.DMA((2,)),
        ],
        compiler_params=pltpu.CompilerParams(
            collective_id=2, has_side_effects=True, vmem_limit_bytes=32 * 2**20),
        name="reduce_parts",
    )(parts)


def piece_kernel(row_ref, col_ref, cell_ref, slot_ref, whole, base, observed, keep,
                 residual_out, adjoint_out, tt, patch, rbuf, spaced):
    piece = pl.program_id(0)

    @pl.when(piece == 0)
    def _():
        tt[...] = jnp.zeros_like(tt)
        rbuf[...] = jnp.zeros_like(rbuf)

    lane = lax.broadcasted_iota(jnp.int32, (PSF, 16, 128), 2)
    kernel = base[0].astype(jnp.float32)
    for j in range(16):
        spaced[pl.ds(j, TAPS, stride=16), :] = pltpu.roll(kernel, j, 1) if j else kernel
    taps = spaced[0 : PSF * 16].reshape(PSF, 16, 128)
    for step in range(B // 16):
        first = 16 * step
        turned = pltpu.roll(taps, first, 2) if first else taps
        over = first + 56 - 128
        if over > 0:
            low = jnp.where(lane >= first, turned, 0.0)
            high = jnp.where(lane < over, turned, 0.0)
            tt[0:PSF, first : first + 16, 128:256] = high.astype(jnp.bfloat16)
        else:
            low = turned
        tt[0:PSF, first : first + 16, 0:128] = low.astype(jnp.bfloat16)

    row0 = pl.multiple_of(row_ref[piece], 128)
    col0 = pl.multiple_of(col_ref[piece], 128)
    window = whole[pl.ds(row0, 192), pl.ds(col0, 384)].astype(jnp.float32)
    shifted = window[ROWPAD - HALO : ROWPAD - HALO + AROWS]
    shifted = pltpu.roll(shifted, 384 - (COLPAD - HALO), 1)[:, 0:256]
    patch[...] = shifted.astype(jnp.bfloat16)

    total = None
    for s in range(14, -1, -2):
        acc = None
        for q in range(3):
            a = 16 * q + s
            if a >= PSF:
                continue
            band = tt[a : a + 2].reshape(256, 256)
            term = lax.dot_general(patch[16 * q : 16 * q + 144, :], band,
                                   (((1,), (1,)), ((), ())), preferred_element_type=jnp.float32)
            acc = term if acc is None else acc + term
        if total is None:
            total = acc[:, 128:256]
        else:
            total = pltpu.roll(total, 143, 0) + acc[:, 128:256]
        total = pltpu.roll(total, 143, 0) + acc[:, 0:128]
    predicted = total[0:B]
    residual = (keep[0].astype(jnp.float32) * (predicted - observed[0].astype(jnp.float32)))
    residual = residual.astype(jnp.bfloat16)
    residual_out[0] = residual
    wide = jnp.concatenate([residual.astype(jnp.float32), jnp.zeros((16, B), jnp.float32)], 0)
    rbuf[32 : 32 + B, 0:128] = residual
    rbuf[32 : 32 + B + 16, 128:256] = pltpu.roll(wide, 1, 0).astype(jnp.bfloat16)

    back = None
    for s in range(14, -1, -2):
        acc = None
        for q in range(3):
            a = 16 * q + s
            if a >= PSF:
                continue
            band = tt[a : a + 2].reshape(256, 256)
            term = jnp.dot(rbuf[32 - 16 * q : 32 - 16 * q + AROWS, :], band,
                           preferred_element_type=jnp.float32)
            acc = term if acc is None else acc + term
        back = acc if back is None else pltpu.roll(back, 2, 0) + acc
    tails = back[0:EXT, 128:256]
    packed = tails[0:FOLD]
    for third in range(1, 3):
        packed = packed + pltpu.roll(tails[third * FOLD : (third + 1) * FOLD], 2 * HALO * third, 1)
    adjoint_out[0] = jnp.concatenate([back[0:EXT, 0:128], packed], 0).astype(jnp.bfloat16)


def run_pieces(rows, cols, cells, slots, whole, base, observed, keep, slot_total):
    count = observed.shape[0]
    flops = count * 21 * 2 * 256 * 256 * (144 + AROWS)
    return pl.pallas_call(
        piece_kernel,
        grid_spec=pltpu.PrefetchScalarGridSpec(
            num_scalar_prefetch=4,
            grid=(count,),
            in_specs=[
                pl.BlockSpec(whole.shape, lambda p, r, c, k, s: (0, 0)),
                pl.BlockSpec((1, TAPS, 128), lambda p, r, c, k, s: (k[p], 0, 0)),
                pl.BlockSpec((1, B, B), lambda p, r, c, k, s: (p, 0, 0)),
                pl.BlockSpec((1, B, B), lambda p, r, c, k, s: (p, 0, 0)),
            ],
            out_specs=[
                pl.BlockSpec((1, B, B), lambda p, r, c, k, s: (p, 0, 0)),
                pl.BlockSpec((1, PACKED, B), lambda p, r, c, k, s: (s[p], 0, 0)),
            ],
            scratch_shapes=[
                pltpu.VMEM((TAPS, B, 256), jnp.bfloat16),
                pltpu.VMEM((AROWS, 256), jnp.bfloat16),
                pltpu.VMEM((32 + AROWS, 256), jnp.bfloat16),
                pltpu.VMEM((TAPS * 16, 128), jnp.float32),
            ],
        ),
        out_shape=[
            jax.ShapeDtypeStruct((count, B, B), jnp.bfloat16),
            jax.ShapeDtypeStruct((slot_total, PACKED, B), jnp.bfloat16),
        ],
        compiler_params=pltpu.CompilerParams(vmem_limit_bytes=56 * 2**20),
        cost_estimate=pl.CostEstimate(flops=flops, bytes_accessed=16 * 2**20, transcendentals=0),
        name="pieces",
    )(rows, cols, cells, slots, whole, base, observed, keep)


def shards(sky_model, exposure_data, pixel_mask, block_owner, block_local, psf_cell, psf_table):
    sky_count = lax.axis_size("sky")
    exp_count = lax.axis_size("exp")
    stripe_rows, stripe_cols = sky_model.shape
    per_row = stripe_cols // B
    block_rows = stripe_rows // B
    piece_count = exposure_data.shape[0]
    slot_total = sky_count * CAP
    owner_sky = block_owner[:, 0]
    index = lax.broadcasted_iota(jnp.int32, (piece_count, piece_count), 0)
    earlier = lax.broadcasted_iota(jnp.int32, (piece_count, piece_count), 1) < index
    same_owner = owner_sky[:, None] == owner_sky[None, :]
    rank_within = jnp.sum((same_owner & earlier).astype(jnp.int32), axis=1)
    slot_index = owner_sky * CAP + rank_within
    named = slot_index[None, :] == lax.broadcasted_iota(jnp.int32, (slot_total, piece_count), 0)
    requests = jnp.sum(jnp.where(named, block_local[None, :] + 1, 0), axis=1) - 1
    requests = requests.reshape(sky_count, 1, CAP)
    requests = jnp.pad(requests, ((0, 0), (0, 7), (0, 128 - CAP)))
    cell_count = psf_table.shape[0]
    kernels = psf_table.reshape(cell_count, PSF, PSF)
    kernels = jnp.pad(kernels, ((0, 0), (0, TAPS - PSF), (0, 128 - PSF)))

    whole = gather_model(sky_model)
    row_start = (owner_sky * block_rows + block_local // per_row) * B
    col_start = block_local % per_row * B
    residuals, adjoints = run_pieces(
        row_start, col_start, psf_cell, slot_index, whole, kernels, exposure_data, pixel_mask, slot_total
    )
    received, asked = exchange(adjoints.reshape(sky_count, CAP, PACKED, B), requests)
    ids = asked[:, 0, :CAP].reshape(slot_total)
    parts = fold(ids, received.reshape(slot_total, PACKED, B), stripe_rows, stripe_cols, exp_count)
    return (reduce_parts(parts), residuals)


def solution(mesh):
    in_specs = (
        P("sky", None),
        P(("sky", "exp"), None, None),
        P(("sky", "exp"), None, None),
        P(("sky", "exp"), None),
        P(("sky", "exp")),
        P(("sky", "exp")),
        P("exp", None),
    )
    out_specs = (P("sky", "exp"), P(("sky", "exp"), None, None))
    return jax.shard_map(shards, mesh=mesh, in_specs=in_specs, out_specs=out_specs, check_vma=False)
```

time: 209 us -> 123 us (0.59)
  waiting for transfers between devices: 97.6 us -> 0 us
  Pallas kernels: 32.1 us -> 114 us
  local copies, waits for them, and re-layouts: 37 us -> 6.39 us
  starting transfers between devices: 16 us -> 0 us
  between operations: 14.3 us -> 0.71 us
  other arithmetic: 9.75 us -> 2.29 us
    pallas_call x0 -> x4, Pallas kernels: none -> 73.9 us  [the longest x1 33.4 us: gather_model(): pl.pallas_call(functools.partial(gather_kernel, count, cuts), out_shape=j...]
    all_gather x1 -> x0, waiting for transfers between devices: 40.9 us -> none  [shards(): whole = lax.all_gather(sky_model, 'sky', axis=0, tiled=True)]
    all_to_all x2 -> x0, waiting for transfers between devices: 29.7 us -> none  [the longest x1 29.7 us: shards(): lax.all_to_all(outgoing, 'sky', split_axis=0, concat_axis=0, tiled=True)]
    another operation x18 -> x1, local copies, waits for them, and re-layouts: 24.6 us -> 0.08 us  [shards(): ids = asked[:, 0, :CAP].reshape(slot_total)]
    reduce_scatter x1 -> x0, waiting for transfers between devices: 22.8 us -> none  [shards(): lax.psum_scatter(folded.astype(jnp.bfloat16), 'exp', scatter_dimension=1,...]
    all_to_all x2 -> x0, starting transfers between devices: 10.3 us -> none  [the longest x1 6.38 us: shards(): lax.all_to_all(requests, 'sky', split_axis=0, concat_axis=0, tiled=True)]
    pallas_call x1, Pallas kernels: 32.1 us -> 39.8 us  [run_pieces(): pl.pallas_call(piece_kernel, grid_spec=pltpu.PrefetchScalarGridSpec(num_s...]
    ppermute x2 -> x0, starting transfers between devices: 5.41 us -> none  [from_behind(): return lax.ppermute(x, axis, pairs)]
  transfers between devices with their start and end apart: 6 -> 0, of which waited for: 4 -> 0; matrix products, arithmetic and copies ran while one was open for 18% -> 0% of each run, Pallas kernels for 15% -> 0%
where the time goes in v2:
time: 123 us
  Pallas kernels  114 us (93%)
  local copies, waits for them, and re-layouts  6.39 us (5%)
  other arithmetic  2.29 us (2%)
    pallas_call x1, Pallas kernels, run_pieces(): pl.pallas_call(piece_kernel, grid_spec=pltpu.PrefetchScalarGridSpec(num_s...  39.8 us
    pallas_call x1, Pallas kernels, gather_model(): pl.pallas_call(functools.partial(gather_kernel, count, cuts), out_shape=j...  33.4 us
    pallas_call x1, Pallas kernels, reduce_parts(): pl.pallas_call(functools.partial(reduce_kernel, skies, exps), out_shape=j...  20.7 us
    pallas_call x1, Pallas kernels, exchange(): pl.pallas_call(functools.partial(exchange_kernel, count), out_shape=[jax....  17.5 us
    unnamed x11, local copies, waits for them, and re-layouts  5.26 us

profile of v2, /device:TPU:1, one launch (start us, length us, event | category | flops | bytes accessed | tf_op | source)
XLA Modules:
  0.0 123.1 jit_solution(7404218420388342442)
XLA Ops:
  0.6 0.9 convert_reduce_fusion
  1.5 1.3 %broadcast_add_fusion.1 = (s32[16]{0:T(128)S(1)}, s32[16]{0:T(128)}, s32[16]{0:T(128)}, s32[16]{0:T(128)}) fusion(s32[16]{0:T(128)} %param.11, s32[16,1]{0,1:T(1,128)} %param.10, s32[16]{0:T(128)S(1)} %convert_reduce_fusion), kind=kLoop, calls=%fused_computation.15 | loop fusion | flops 400 | bytes 448 | tf_op jit(solution)/shard_map/add | solution.py:437
  2.8 0.0 copy-start.2
  2.8 1.0 copy-done.2
  3.8 0.0 copy-start.3
  3.8 33.4 %gather_model.1.whole = bf16[2112,1280]{1,0:T(8,128)(2,1)S(1)} custom-call(bf16[256,1024]{1,0:T(8,128)(2,1)S(1)} %copy-done.2), custom_call_target="tpu_custom_call" | custom-call | tf_op jit(solution)/shard_map/gather_model/pallas_call | solution.py:128
  37.2 0.0 copy-start
  37.2 2.3 %copy-done = bf16[2112,1280]{1,0:T(8,128)(2,1)} copy-done((bf16[2112,1280]{1,0:T(8,128)(2,1)}, bf16[2112,1280]{1,0:T(8,128)(2,1)S(1)}, u32[]{:S(2)}) %copy-start) | copy-done | bytes 5406744
  39.5 0.0 copy-done.3
  39.6 0.2 reshape.37
  39.8 0.7 pad.8.base
  40.5 0.0 copy-start.4
  40.5 39.8 %pieces.1 = (bf16[16,128,128]{2,1,0:T(8,128)(2,1)}, bf16[16,224,128]{2,1,0:T(8,128)(2,1)}) custom-call(s32[16]{0:T(128)} %get-tuple-element.11.row_ref, s32[16]{0:T(128)} %get-tuple-element.13.col_ref, s32[16]{0:T(128)} %cell_ref.1, s32[16]{0:T(128)} %get-tuple-element.12.slot_ref, bf16[2112,1280]{1,0:T(8,128)(2,1)} %copy-done, ...), custom_call_target="tpu_custom_call" | custom-call | flops 14092861440 | bytes 16777216 | tf_op jit(solution)/shard_map/pieces/pallas_call | solution.py:390
  80.3 0.0 copy-done.4
  80.3 0.1 select_reduce_fusion
  80.4 0.1 sub.11
  80.5 0.0 copy-start.1
  80.5 1.2 copy-done.1
  81.7 17.5 %exchange.1 = (bf16[8,2,224,128]{3,2,1,0:T(8,128)(2,1)S(1)}, s32[8,8,128]{2,1,0:T(8,128)S(1)}) custom-call(bf16[8,2,224,128]{3,2,1,0:T(8,128)(2,1)S(1)} %bitcast.6, s32[8,8,128]{2,1,0:T(8,128)S(1)} %pad.9.asked), custom_call_target="tpu_custom_call" | custom-call | tf_op jit(solution)/shard_map/exchange/pallas_call | solution.py:174
  99.2 0.1 reshape_squeeze.3.ids
  99.3 2.4 %fold.1.parts = bf16[4,320,256]{2,1,0:T(8,128)(2,1)S(1)} custom-call(s32[16]{0:T(128)S(1)} %reshape_squeeze.3.ids, bf16[16,224,128]{2,1,0:T(8,128)(2,1)S(1)} %bitcast.7), custom_call_target="tpu_custom_call" | custom-call | tf_op jit(solution)/shard_map/fold/pallas_call | solution.py:222
  101.7 20.7 %reduce_parts.1 = f32[256,256]{1,0:T(8,128)S(1)} custom-call(bf16[4,320,256]{2,1,0:T(8,128)(2,1)S(1)} %fold.1.parts), custom_call_target="tpu_custom_call" | custom-call | tf_op jit(solution)/shard_map/reduce_parts/pallas_call | solution.py:291
  122.4 0.7 copy.13
  (3 shorter events, 0.0 us)
Async XLA Ops:
  2.8 1.0 copy-start.2
  3.8 35.7 %copy-start.3 = (bf16[16,1681]{1,0:T(8,128)(2,1)S(1)}, bf16[16,1681]{1,0:T(8,128)(2,1)}, u32[]{:S(2)}) copy-start(bf16[16,1681]{1,0:T(8,128)(2,1)} %param.13) | copy-start | bytes 161380
  37.2 2.3 %copy-start = (bf16[2112,1280]{1,0:T(8,128)(2,1)}, bf16[2112,1280]{1,0:T(8,128)(2,1)S(1)}, u32[]{:S(2)}) copy-start(bf16[2112,1280]{1,0:T(8,128)(2,1)S(1)} %gather_model.1.whole) | copy-start | bytes 16220164
  40.5 39.8 %copy-start.4 = (s32[16]{0:T(128)S(1)}, s32[16]{0:T(128)}, u32[]{:S(2)}) copy-start(s32[16]{0:T(128)} %get-tuple-element.12.slot_ref) | copy-start | bytes 196
  80.5 1.2 copy-start.1

commit v3 on v2

--- a/solution.py
+++ b/solution.py
@@ -34,54 +34,61 @@
     return 2 * place * (1 - late) + (2 * (count - 1 - place) + 1) * late
 
 
-def gather_kernel(count, cuts, stripe, whole, zero, ring_send, ring_recv, pair_send, pair_recv, local_sem):
+def gather_kernel(count, cuts, stripe, kernels, whole, table, zero, spaced, bands, ring_send, ring_recv,
+                  pair_send, pair_recv, cross_send, cross_recv, last_send, last_recv, local_sem, table_sem):
     sky = lax.axis_index("sky")
     own = lax.axis_index("exp")
     core = own % 2
+    half = (own % 4) // 2
     pair = own + 1 - 2 * core
+    cross = own + 2 - 4 * half
     place = ring_place(sky, count)
     ahead = ring_sky((place + 1) % count, count)
     behind = ring_sky((place + count - 1) % count, count)
     rows, cols = stripe.shape
-    part = rows // (4 * cuts)
+    cells = kernels.shape[0]
+    part = rows // (8 * cuts)
+    quarter, other = core + 2 * half, core + 2 * (1 - half)
 
     barrier = pltpu.get_barrier_semaphore()
-    for target in ((ahead, own), (behind, own), (sky, pair)):
+    for target in ((ahead, own), (behind, own), (sky, pair), (sky, cross)):
         pl.semaphore_signal(barrier, inc=1, device_id=target, device_id_type=MESH)
-    pl.semaphore_wait(barrier, 3)
-
-    def inner(way, cut):
-        return core * (rows // 2) + way * (rows // 4) + cut * part
-
-    def spot(origin, way, cut):
-        first = pl.multiple_of(ROWPAD + origin * rows + inner(way, cut), 16)
+    pl.semaphore_wait(barrier, 4)
+
+    def inner(share, way, cut):
+        return share * (rows // 4) + way * (rows // 8) + cut * part
+
+    def spot(share, step, way, cut):
+        origin = ring_sky((place + count - (1 - 2 * way) * step) % count, count)
+        first = pl.multiple_of(ROWPAD + origin * rows + inner(share, way, cut), 16)
         return whole.at[pl.ds(first, part), pl.ds(COLPAD, cols)]
 
-    def ring_copy(step, way, cut):
-        sign = 1 - 2 * way
-        origin = ring_sky((place + count - sign * step) % count, count)
-        if step == 0:
-            block = stripe.at[pl.ds(pl.multiple_of(inner(way, cut), 16), part), :]
-        else:
-            block = spot(origin, way, cut)
+    def ring_copy(step, way, cut, first=False):
+        dest = spot(quarter, step, way, cut)
+        source = stripe.at[pl.ds(pl.multiple_of(inner(quarter, way, cut), 16), part), :] if first else dest
         return pltpu.make_async_remote_copy(
-            src_ref=block, dst_ref=spot(origin, way, cut),
+            src_ref=source, dst_ref=dest,
             send_sem=ring_send.at[step, way, cut], recv_sem=ring_recv.at[step, way, cut],
             device_id=((behind if way else ahead), own), device_id_type=MESH)
 
+    def hand_on(share, step, way, cut, send, recv, target):
+        block = spot(share, step, way, cut)
+        return pltpu.make_async_remote_copy(
+            src_ref=block, dst_ref=block, send_sem=send.at[step - 1, way, cut],
+            recv_sem=recv.at[step - 1, way, cut], device_id=(sky, target), device_id_type=MESH)
+
     def pair_copy(step, way, cut):
-        sign = 1 - 2 * way
-        origin = ring_sky((place + count - sign * step) % count, count)
-        return pltpu.make_async_remote_copy(
-            src_ref=spot(origin, way, cut), dst_ref=spot(origin, way, cut),
-            send_sem=pair_send.at[step - 1, way, cut], recv_sem=pair_recv.at[step - 1, way, cut],
-            device_id=(sky, pair), device_id_type=MESH)
-
-    sends, pairs = {}, []
-    for cut in range(cuts):
-        for way in range(2):
-            sends[0, way, cut] = ring_copy(0, way, cut)
-            sends[0, way, cut].start()
+        return hand_on(quarter, step, way, cut, pair_send, pair_recv, pair)
+
+    def cross_copy(step, way, cut):
+        return hand_on(quarter, step, way, cut, cross_send, cross_recv, cross)
+
+    def last_copy(step, way, cut):
+        return hand_on(other, step, way, cut, last_send, last_recv, pair)
+
+    each = [(cut, way) for cut in range(cuts) for way in range(2)]
+    for cut, way in each:
+        ring_copy(0, way, cut, True).start()
 
     zero[...] = jnp.zeros_like(zero)
     total = whole.shape[0]
@@ -100,48 +107,118 @@
     for fill in fills:
         fill.start()
 
-    for step in range(1, count):
+    for slot in range(2):
+        bands[slot, PSF] = jnp.zeros((B, 256), bands.dtype)
+        bands[slot, 0:PSF, :, 128:256] = jnp.zeros((PSF, B, 128), bands.dtype)
+
+    def table_copy(cell, slot):
+        return pltpu.make_async_copy(bands.at[slot], table.at[cell], table_sem.at[slot])
+
+    def build(cell):
+        slot = cell % 2
+
+        @pl.when(cell >= 2)
+        def _():
+            table_copy(cell, slot).wait()
+
+        kernel = kernels[cell].astype(jnp.float32)
+        for j in range(16):
+            spaced[pl.ds(j, TAPS, stride=16), :] = pltpu.roll(kernel, j, 1) if j else kernel
+        taps = spaced[0 : PSF * 16].reshape(PSF, 16, 128)
+        lane = lax.broadcasted_iota(jnp.int32, (PSF, 16, 128), 2)
+        for step in range(B // 16):
+            first = 16 * step
+            turned = pltpu.roll(taps, first, 2) if first else taps
+            over = first + 56 - 128
+            if over > 0:
+                low = jnp.where(lane >= first, turned, 0.0)
+                high = jnp.where(lane < over, turned, 0.0)
+                bands[slot, 0:PSF, first : first + 16, 128:256] = high.astype(jnp.bfloat16)
+            else:
+                low = turned
+            bands[slot, 0:PSF, first : first + 16, 0:128] = low.astype(jnp.bfloat16)
+        table_copy(cell, slot).start()
+
+    early = max(0, cells - (count - 1) * cuts)
+
+    def build_early(cell, carry):
+        build(cell)
+        return carry
+
+    lax.fori_loop(0, early, build_early, 0)
+
+    def ring_step(step, carry):
         for cut in range(cuts):
             for way in range(2):
-                sends[step - 1, way, cut].wait_recv()
-                if step < count - 1:
-                    sends[step, way, cut] = ring_copy(step, way, cut)
-                    sends[step, way, cut].start()
-                extra = pair_copy(step, way, cut)
-                extra.start()
-                pairs.append((step, way, cut, extra))
-    for copy in sends.values():
-        copy.wait_send()
-    for step, way, cut, extra in pairs:
-        extra.wait_send()
-        extra.wait_recv()
+                ring_copy(step - 1, way, cut).wait_recv()
+
+                @pl.when(step < count - 1)
+                def _():
+                    ring_copy(step, way, cut).start()
+
+                cross_copy(step, way, cut).start()
+                pair_copy(step, way, cut).start()
+
+                @pl.when(step > 1)
+                def _():
+                    cross_copy(step - 1, way, cut).wait_recv()
+                    last_copy(step - 1, way, cut).start()
+
+            cell = early + (step - 1) * cuts + cut
+
+            @pl.when(cell < cells)
+            def _():
+                build(cell)
+
+        return carry
+
+    lax.fori_loop(1, count, ring_step, 0)
+    for cut, way in each:
+        cross_copy(count - 1, way, cut).wait_recv()
+        last_copy(count - 1, way, cut).start()
+
+    def drain(step, carry):
+        for cut, way in each:
+            ring_copy(step - 1, way, cut).wait_send()
+            cross_copy(step, way, cut).wait_send()
+            pair_copy(step, way, cut).wait()
+            last_copy(step, way, cut).wait()
+        return carry
+
+    lax.fori_loop(1, count, drain, 0)
     for fill in fills:
         fill.wait()
-
-
-def gather_model(stripe):
+    for cell in range(cells - 2, cells):
+        table_copy(cell, cell % 2).wait()
+
+
+def gather_model(stripe, kernels):
     count = lax.axis_size("sky")
     rows, cols = stripe.shape
+    cells = kernels.shape[0]
     cuts = 2
     shape = (count * rows + 2 * ROWPAD, cols + 2 * COLPAD)
     steps = (count - 1, 2, cuts)
     return pl.pallas_call(
         functools.partial(gather_kernel, count, cuts),
-        out_shape=jax.ShapeDtypeStruct(shape, stripe.dtype),
-        in_specs=[pl.BlockSpec(memory_space=pl.ANY)],
-        out_specs=pl.BlockSpec(memory_space=pl.ANY),
+        out_shape=[
+            jax.ShapeDtypeStruct(shape, stripe.dtype),
+            jax.ShapeDtypeStruct((cells, PSF + 1, B, 256), jnp.bfloat16),
+        ],
+        in_specs=[pl.BlockSpec(memory_space=pl.ANY), pl.BlockSpec(memory_space=pltpu.VMEM)],
+        out_specs=[pl.BlockSpec(memory_space=pl.ANY)] * 2,
         scratch_shapes=[
             pltpu.VMEM((shape[0], COLPAD), stripe.dtype),
-            pltpu.SemaphoreType.DMA(steps),
-            pltpu.SemaphoreType.DMA(steps),
-            pltpu.SemaphoreType.DMA(steps),
-            pltpu.SemaphoreType.DMA(steps),
+            pltpu.VMEM((TAPS * 16, 128), jnp.float32),
+            pltpu.VMEM((2, PSF + 1, B, 256), jnp.bfloat16),
+        ] + [pltpu.SemaphoreType.DMA(steps)] * 8 + [
             pltpu.SemaphoreType.DMA((3 + 2 * (cols // COLPAD),)),
+            pltpu.SemaphoreType.DMA((2,)),
         ],
         compiler_params=pltpu.CompilerParams(
-            collective_id=0, has_side_effects=True, vmem_limit_bytes=32 * 2**20),
+            collective_id=0, has_side_effects=True, vmem_limit_bytes=48 * 2**20),
         name="gather_model",
-    )(stripe)
+    )(stripe, kernels)
 
 
 def exchange_kernel(count, data, asked, got, got_asked, data_send, data_recv, id_send, id_recv, local_sem):
@@ -308,35 +385,28 @@
     )(parts)
 
 
-def piece_kernel(row_ref, col_ref, cell_ref, slot_ref, whole, base, observed, keep,
-                 residual_out, adjoint_out, tt, patch, rbuf, spaced):
+def piece_kernel(row_ref, col_ref, cell_ref, slot_ref, whole, bands, observed, keep,
+                 residual_out, adjoint_out, windows, patch, rbuf, window_sem):
     piece = pl.program_id(0)
+    tt = bands.at[0]
+
+    def fetch(index):
+        row0 = pl.multiple_of(row_ref[index], 128)
+        col0 = pl.multiple_of(col_ref[index], 128)
+        return pltpu.make_async_copy(
+            whole.at[pl.ds(row0, 192), pl.ds(col0, 384)], windows.at[index % 2], window_sem.at[index % 2])
 
     @pl.when(piece == 0)
     def _():
-        tt[...] = jnp.zeros_like(tt)
         rbuf[...] = jnp.zeros_like(rbuf)
-
-    lane = lax.broadcasted_iota(jnp.int32, (PSF, 16, 128), 2)
-    kernel = base[0].astype(jnp.float32)
-    for j in range(16):
-        spaced[pl.ds(j, TAPS, stride=16), :] = pltpu.roll(kernel, j, 1) if j else kernel
-    taps = spaced[0 : PSF * 16].reshape(PSF, 16, 128)
-    for step in range(B // 16):
-        first = 16 * step
-        turned = pltpu.roll(taps, first, 2) if first else taps
-        over = first + 56 - 128
-        if over > 0:
-            low = jnp.where(lane >= first, turned, 0.0)
-            high = jnp.where(lane < over, turned, 0.0)
-            tt[0:PSF, first : first + 16, 128:256] = high.astype(jnp.bfloat16)
-        else:
-            low = turned
-        tt[0:PSF, first : first + 16, 0:128] = low.astype(jnp.bfloat16)
-
-    row0 = pl.multiple_of(row_ref[piece], 128)
-    col0 = pl.multiple_of(col_ref[piece], 128)
-    window = whole[pl.ds(row0, 192), pl.ds(col0, 384)].astype(jnp.float32)
+        fetch(0).start()
+
+    @pl.when(piece + 1 < pl.num_programs(0))
+    def _():
+        fetch(piece + 1).start()
+
+    fetch(piece).wait()
+    window = windows[piece % 2].astype(jnp.float32)
     shifted = window[ROWPAD - HALO : ROWPAD - HALO + AROWS]
     shifted = pltpu.roll(shifted, 384 - (COLPAD - HALO), 1)[:, 0:256]
     patch[...] = shifted.astype(jnp.bfloat16)
@@ -393,8 +463,8 @@
             num_scalar_prefetch=4,
             grid=(count,),
             in_specs=[
-                pl.BlockSpec(whole.shape, lambda p, r, c, k, s: (0, 0)),
-                pl.BlockSpec((1, TAPS, 128), lambda p, r, c, k, s: (k[p], 0, 0)),
+                pl.BlockSpec(memory_space=pl.ANY),
+                pl.BlockSpec((1, PSF + 1, B, 256), lambda p, r, c, k, s: (k[p], 0, 0, 0)),
                 pl.BlockSpec((1, B, B), lambda p, r, c, k, s: (p, 0, 0)),
                 pl.BlockSpec((1, B, B), lambda p, r, c, k, s: (p, 0, 0)),
             ],
@@ -403,10 +473,10 @@
                 pl.BlockSpec((1, PACKED, B), lambda p, r, c, k, s: (s[p], 0, 0)),
             ],
             scratch_shapes=[
-                pltpu.VMEM((TAPS, B, 256), jnp.bfloat16),
+                pltpu.VMEM((2, 192, 384), jnp.bfloat16),
                 pltpu.VMEM((AROWS, 256), jnp.bfloat16),
                 pltpu.VMEM((32 + AROWS, 256), jnp.bfloat16),
-                pltpu.VMEM((TAPS * 16, 128), jnp.float32),
+                pltpu.SemaphoreType.DMA((2,)),
             ],
         ),
         out_shape=[
@@ -441,11 +511,11 @@
     kernels = psf_table.reshape(cell_count, PSF, PSF)
     kernels = jnp.pad(kernels, ((0, 0), (0, TAPS - PSF), (0, 128 - PSF)))
 
-    whole = gather_model(sky_model)
+    whole, table = gather_model(sky_model, kernels)
     row_start = (owner_sky * block_rows + block_local // per_row) * B
     col_start = block_local % per_row * B
     residuals, adjoints = run_pieces(
-        row_start, col_start, psf_cell, slot_index, whole, kernels, exposure_data, pixel_mask, slot_total
+        row_start, col_start, psf_cell, slot_index, whole, table, exposure_data, pixel_mask, slot_total
     )
     received, asked = exchange(adjoints.reshape(sky_count, CAP, PACKED, B), requests)
     ids = asked[:, 0, :CAP].reshape(slot_total)

time: 123 us -> 117 us (0.951)
  Pallas kernels: 114 us -> 107 us
    pallas_call x1, Pallas kernels: 39.8 us -> 32.5 us  [run_pieces(): pl.pallas_call(piece_kernel, grid_spec=pltpu.PrefetchScalarGridSpec(num_s...]
    unnamed x11 -> x9, local copies, waits for them, and re-layouts: 5.26 us -> 5.28 us
where the time goes in v3:
time: 117 us; the launch traced here: 116 us
  Pallas kernels  107 us (91%)
  local copies, waits for them, and re-layouts  6.57 us (6%)
  other arithmetic  2.31 us (2%)
    pallas_call x1, Pallas kernels, gather_model(): pl.pallas_call(functools.partial(gather_kernel, count, cuts), out_shape=[...  33.8 us
    pallas_call x1, Pallas kernels, run_pieces(): pl.pallas_call(piece_kernel, grid_spec=pltpu.PrefetchScalarGridSpec(num_s...  32.5 us
    pallas_call x1, Pallas kernels, reduce_parts(): pl.pallas_call(functools.partial(reduce_kernel, skies, exps), out_shape=j...  20.7 us
    pallas_call x1, Pallas kernels, exchange(): pl.pallas_call(functools.partial(exchange_kernel, count), out_shape=[jax....  17.5 us
    unnamed x9, local copies, waits for them, and re-layouts  5.28 us
    pallas_call x1, Pallas kernels, fold(): pl.pallas_call(functools.partial(fold_kernel, stripe_rows, stripe_cols, e...  2.39 us

profile of v3, /device:TPU:1, one launch (start us, length us, event | category | flops | bytes accessed | tf_op | source)
XLA Modules:
  0.0 116.5 jit_solution(6458597993437690441)
XLA Ops:
  0.6 0.9 convert_reduce_fusion
  1.5 1.3 %broadcast_add_fusion.1 = (s32[16]{0:T(128)S(1)}, s32[16]{0:T(128)}, s32[16]{0:T(128)}, s32[16]{0:T(128)}) fusion(s32[16]{0:T(128)} %param.11, s32[16,1]{0,1:T(1,128)} %param.10, s32[16]{0:T(128)S(1)} %convert_reduce_fusion), kind=kLoop, calls=%fused_computation.15 | loop fusion | flops 400 | bytes 448 | tf_op jit(solution)/shard_map/add | solution.py:507
  2.8 0.0 copy-start.3
  2.8 1.1 reshape.37
  3.9 0.0 copy-start.1
  3.9 1.0 copy-done.1
  5.0 33.8 %gather_model.1 = (bf16[2112,1280]{1,0:T(8,128)(2,1)S(1)}, bf16[16,42,128,256]{3,2,1,0:T(8,128)(2,1)}) custom-call(bf16[256,1024]{1,0:T(8,128)(2,1)S(1)} %copy-done.1, bf16[16,48,128]{2,1,0:T(8,128)(2,1)S(1)} %pad.8.kernels), custom_call_target="tpu_custom_call" | custom-call | tf_op jit(solution)/shard_map/gather_model/pallas_call | solution.py:202
  38.8 0.0 copy-start.2
  38.8 2.4 %copy-done.2 = bf16[2112,1280]{1,0:T(8,128)(2,1)} copy-done((bf16[2112,1280]{1,0:T(8,128)(2,1)}, bf16[2112,1280]{1,0:T(8,128)(2,1)S(1)}, u32[]{:S(2)}) %copy-start.2) | copy-done | bytes 5406744
  41.2 32.5 %pieces.1 = (bf16[16,128,128]{2,1,0:T(8,128)(2,1)}, bf16[16,224,128]{2,1,0:T(8,128)(2,1)}) custom-call(s32[16]{0:T(128)} %get-tuple-element.15.row_ref, s32[16]{0:T(128)} %get-tuple-element.17.col_ref, s32[16]{0:T(128)} %cell_ref.1, s32[16]{0:T(128)} %get-tuple-element.16.slot_ref, bf16[2112,1280]{1,0:T(8,128)(2,1)} %copy-done.2, ...), custom_call_target="tpu_custom_call" | custom-call | flops 14092861440 | bytes 16777216 | tf_op jit(solution)/shard_map/pieces/pallas_call | solution.py:460
  73.7 0.0 copy-done.3
  73.7 0.1 select_reduce_fusion
  73.8 0.1 sub.11
  73.9 0.0 copy-start
  73.9 1.2 %copy-done = bf16[16,224,128]{2,1,0:T(8,128)(2,1)S(1)} copy-done((bf16[16,224,128]{2,1,0:T(8,128)(2,1)S(1)}, bf16[16,224,128]{2,1,0:T(8,128)(2,1)}, u32[]{:S(2)}) %copy-start) | copy-done | bytes 917528
  75.1 17.5 %exchange.1 = (bf16[8,2,224,128]{3,2,1,0:T(8,128)(2,1)S(1)}, s32[8,8,128]{2,1,0:T(8,128)S(1)}) custom-call(bf16[8,2,224,128]{3,2,1,0:T(8,128)(2,1)S(1)} %bitcast.6, s32[8,8,128]{2,1,0:T(8,128)S(1)} %pad.9.asked), custom_call_target="tpu_custom_call" | custom-call | tf_op jit(solution)/shard_map/exchange/pallas_call | solution.py:251
  92.6 0.1 reshape_squeeze.3.ids
  92.7 2.4 %fold.1.parts = bf16[4,320,256]{2,1,0:T(8,128)(2,1)S(1)} custom-call(s32[16]{0:T(128)S(1)} %reshape_squeeze.3.ids, bf16[16,224,128]{2,1,0:T(8,128)(2,1)S(1)} %bitcast.7), custom_call_target="tpu_custom_call" | custom-call | tf_op jit(solution)/shard_map/fold/pallas_call | solution.py:299
  95.1 20.7 %reduce_parts.1 = f32[256,256]{1,0:T(8,128)S(1)} custom-call(bf16[4,320,256]{2,1,0:T(8,128)(2,1)S(1)} %fold.1.parts), custom_call_target="tpu_custom_call" | custom-call | tf_op jit(solution)/shard_map/reduce_parts/pallas_call | solution.py:368
  115.8 0.7 copy.13
  (4 shorter events, 0.1 us)
Async XLA Ops:
  2.8 70.9 %copy-start.3 = (s32[16]{0:T(128)S(1)}, s32[16]{0:T(128)}, u32[]{:S(2)}) copy-start(s32[16]{0:T(128)} %get-tuple-element.16.slot_ref) | copy-start | bytes 196
  3.9 1.0 copy-start.1
  38.8 2.4 %copy-start.2 = (bf16[2112,1280]{1,0:T(8,128)(2,1)}, bf16[2112,1280]{1,0:T(8,128)(2,1)S(1)}, u32[]{:S(2)}) copy-start(bf16[2112,1280]{1,0:T(8,128)(2,1)S(1)} %get-tuple-element.8.whole) | copy-start | bytes 16220164
  73.9 1.2 %copy-start = (bf16[16,224,128]{2,1,0:T(8,128)(2,1)S(1)}, bf16[16,224,128]{2,1,0:T(8,128)(2,1)}, u32[]{:S(2)}) copy-start(bf16[16,224,128]{2,1,0:T(8,128)(2,1)} %get-tuple-element.10) | copy-start | bytes 2752516

commit v4 on v3

--- a/solution.py
+++ b/solution.py
@@ -107,10 +107,6 @@
     for fill in fills:
         fill.start()
 
-    for slot in range(2):
-        bands[slot, PSF] = jnp.zeros((B, 256), bands.dtype)
-        bands[slot, 0:PSF, :, 128:256] = jnp.zeros((PSF, B, 128), bands.dtype)
-
     def table_copy(cell, slot):
         return pltpu.make_async_copy(bands.at[slot], table.at[cell], table_sem.at[slot])
 
@@ -124,19 +120,7 @@
         kernel = kernels[cell].astype(jnp.float32)
         for j in range(16):
             spaced[pl.ds(j, TAPS, stride=16), :] = pltpu.roll(kernel, j, 1) if j else kernel
-        taps = spaced[0 : PSF * 16].reshape(PSF, 16, 128)
-        lane = lax.broadcasted_iota(jnp.int32, (PSF, 16, 128), 2)
-        for step in range(B // 16):
-            first = 16 * step
-            turned = pltpu.roll(taps, first, 2) if first else taps
-            over = first + 56 - 128
-            if over > 0:
-                low = jnp.where(lane >= first, turned, 0.0)
-                high = jnp.where(lane < over, turned, 0.0)
-                bands[slot, 0:PSF, first : first + 16, 128:256] = high.astype(jnp.bfloat16)
-            else:
-                low = turned
-            bands[slot, 0:PSF, first : first + 16, 0:128] = low.astype(jnp.bfloat16)
+        bands[slot] = spaced[0 : PSF * 16].astype(jnp.bfloat16)
         table_copy(cell, slot).start()
 
     early = max(0, cells - (count - 1) * cuts)
@@ -203,14 +187,14 @@
         functools.partial(gather_kernel, count, cuts),
         out_shape=[
             jax.ShapeDtypeStruct(shape, stripe.dtype),
-            jax.ShapeDtypeStruct((cells, PSF + 1, B, 256), jnp.bfloat16),
+            jax.ShapeDtypeStruct((cells, PSF * 16, 128), jnp.bfloat16),
         ],
         in_specs=[pl.BlockSpec(memory_space=pl.ANY), pl.BlockSpec(memory_space=pltpu.VMEM)],
         out_specs=[pl.BlockSpec(memory_space=pl.ANY)] * 2,
         scratch_shapes=[
             pltpu.VMEM((shape[0], COLPAD), stripe.dtype),
             pltpu.VMEM((TAPS * 16, 128), jnp.float32),
-            pltpu.VMEM((2, PSF + 1, B, 256), jnp.bfloat16),
+            pltpu.VMEM((2, PSF * 16, 128), jnp.bfloat16),
         ] + [pltpu.SemaphoreType.DMA(steps)] * 8 + [
             pltpu.SemaphoreType.DMA((3 + 2 * (cols // COLPAD),)),
             pltpu.SemaphoreType.DMA((2,)),
@@ -221,46 +205,7 @@
     )(stripe, kernels)
 
 
-def exchange_kernel(count, data, asked, got, got_asked, data_send, data_recv, id_send, id_recv, local_sem):
-    sky = lax.axis_index("sky")
-    own = lax.axis_index("exp")
-    barrier = pltpu.get_barrier_semaphore()
-    for turn in range(1, count):
-        pl.semaphore_signal(barrier, inc=1, device_id=((sky + turn) % count, own), device_id_type=MESH)
-    pl.semaphore_wait(barrier, count - 1)
-    copies = []
-    for turn in range(1, count):
-        target = (sky + turn) % count
-        for source, dest, send, recv in ((data, got, data_send, data_recv), (asked, got_asked, id_send, id_recv)):
-            copy = pltpu.make_async_remote_copy(
-                src_ref=source.at[target], dst_ref=dest.at[sky],
-                send_sem=send.at[turn - 1], recv_sem=recv.at[turn - 1],
-                device_id=(target, own), device_id_type=MESH)
-            copy.start()
-            copies.append(copy)
-    for place, (source, dest) in enumerate(((data, got), (asked, got_asked))):
-        copy = pltpu.make_async_copy(source.at[sky], dest.at[sky], local_sem.at[place])
-        copy.start()
-        copies.append(copy)
-    for copy in copies:
-        copy.wait()
-
-
-def exchange(data, asked):
-    count = lax.axis_size("sky")
-    return pl.pallas_call(
-        functools.partial(exchange_kernel, count),
-        out_shape=[jax.ShapeDtypeStruct(x.shape, x.dtype) for x in (data, asked)],
-        in_specs=[pl.BlockSpec(memory_space=pl.ANY)] * 2,
-        out_specs=[pl.BlockSpec(memory_space=pl.ANY)] * 2,
-        scratch_shapes=[pltpu.SemaphoreType.DMA((count - 1,))] * 4 + [pltpu.SemaphoreType.DMA((2,))],
-        compiler_params=pltpu.CompilerParams(
-            collective_id=1, has_side_effects=True, vmem_limit_bytes=32 * 2**20),
-        name="exchange",
-    )(data, asked)
-
-
-def fold_kernel(stripe_rows, stripe_cols, exps, ids, parts, out, canvas):
+def fold_kernel(stripe_rows, stripe_cols, exps, ids, slots, parts, by_slot, out, residual_out, canvas):
     per_row = stripe_cols // B
     canvas[...] = jnp.zeros_like(canvas)
     lane = lax.broadcasted_iota(jnp.int32, (FOLD, B), 1)
@@ -284,6 +229,12 @@
         return carry
 
     lax.fori_loop(0, ids.shape[0], add, 0)
+
+    def reorder(piece, carry):
+        residual_out[piece] = by_slot[slots[piece]]
+        return carry
+
+    lax.fori_loop(0, slots.shape[0], reorder, 0)
     width = stripe_cols + B
     middle = pltpu.roll(canvas[...], width - HALO, 1)[:, 0:stripe_cols]
     upper = jnp.concatenate([jnp.zeros((RIM - HALO, stripe_cols), jnp.float32), middle[0:HALO]], 0)
@@ -294,21 +245,31 @@
         out[e] = rows[:, e * share : (e + 1) * share]
 
 
-def fold(ids, parts, stripe_rows, stripe_cols, exps):
+def fold(ids, slots, parts, by_slot, stripe_rows, stripe_cols, exps):
     shape = (exps, stripe_rows + 2 * RIM, stripe_cols // exps)
+    residual_shape = (slots.shape[0], B, B)
     return pl.pallas_call(
         functools.partial(fold_kernel, stripe_rows, stripe_cols, exps),
         grid_spec=pltpu.PrefetchScalarGridSpec(
-            num_scalar_prefetch=1,
+            num_scalar_prefetch=2,
             grid=(1,),
-            in_specs=[pl.BlockSpec(parts.shape, lambda i, ids: (0, 0, 0))],
-            out_specs=pl.BlockSpec(shape, lambda i, ids: (0, 0, 0)),
+            in_specs=[
+                pl.BlockSpec(parts.shape, lambda i, ids, slots: (0, 0, 0)),
+                pl.BlockSpec(by_slot.shape, lambda i, ids, slots: (0, 0, 0)),
+            ],
+            out_specs=[
+                pl.BlockSpec(shape, lambda i, ids, slots: (0, 0, 0)),
+                pl.BlockSpec(residual_shape, lambda i, ids, slots: (0, 0, 0)),
+            ],
             scratch_shapes=[pltpu.VMEM((stripe_rows + 56, stripe_cols + B), jnp.float32)],
         ),
-        out_shape=jax.ShapeDtypeStruct(shape, jnp.bfloat16),
+        out_shape=[
+            jax.ShapeDtypeStruct(shape, jnp.bfloat16),
+            jax.ShapeDtypeStruct(residual_shape, jnp.bfloat16),
+        ],
         compiler_params=pltpu.CompilerParams(vmem_limit_bytes=40 * 2**20),
         name="fold",
-    )(ids, parts)
+    )(ids, slots, parts, by_slot)
 
 
 def reduce_kernel(skies, exps, parts, out, held, rims, rims_in, send, recv, rim_send, rim_recv):
@@ -385,108 +346,187 @@
     )(parts)
 
 
-def piece_kernel(row_ref, col_ref, cell_ref, slot_ref, whole, bands, observed, keep,
-                 residual_out, adjoint_out, windows, patch, rbuf, window_sem):
-    piece = pl.program_id(0)
-    tt = bands.at[0]
-
-    def fetch(index):
-        row0 = pl.multiple_of(row_ref[index], 128)
-        col0 = pl.multiple_of(col_ref[index], 128)
-        return pltpu.make_async_copy(
-            whole.at[pl.ds(row0, 192), pl.ds(col0, 384)], windows.at[index % 2], window_sem.at[index % 2])
-
-    @pl.when(piece == 0)
-    def _():
-        rbuf[...] = jnp.zeros_like(rbuf)
-        fetch(0).start()
-
-    @pl.when(piece + 1 < pl.num_programs(0))
-    def _():
-        fetch(piece + 1).start()
-
-    fetch(piece).wait()
-    window = windows[piece % 2].astype(jnp.float32)
+def piece_kernel(count, asked, patches, base, observed, keep,
+                 residual_out, got, got_asked, outbox, tt, rbuf,
+                 data_send, data_recv, id_send, id_recv, local_sem):
+    sky = lax.axis_index("sky")
+    own = lax.axis_index("exp")
+    barrier = pltpu.get_barrier_semaphore()
+    for turn in range(1, count):
+        pl.semaphore_signal(barrier, inc=1, device_id=((sky + turn) % count, own), device_id_type=MESH)
+    pl.semaphore_wait(barrier, count - 1)
+    copies = []
+    for turn in range(1, count):
+        target = (sky + turn) % count
+        copies.append(pltpu.make_async_remote_copy(
+            src_ref=asked.at[target], dst_ref=got_asked.at[sky],
+            send_sem=id_send.at[turn - 1], recv_sem=id_recv.at[turn - 1],
+            device_id=(target, own), device_id_type=MESH))
+    copies.append(pltpu.make_async_copy(asked.at[sky], got_asked.at[sky], local_sem.at[CAP]))
+    for copy in copies:
+        copy.start()
+
+    def place_of(turn):
+        return ((sky + 1 + turn // CAP) % count) * CAP + turn % CAP
+
+    def send(turn):
+        return pltpu.make_async_remote_copy(
+            src_ref=outbox.at[place_of(turn)], dst_ref=got.at[sky * CAP + turn % CAP],
+            send_sem=data_send.at[turn], recv_sem=data_recv.at[turn],
+            device_id=((sky + 1 + turn // CAP) % count, own), device_id_type=MESH)
+
+    tt[...] = jnp.zeros_like(tt)
+    rbuf[...] = jnp.zeros_like(rbuf)
+    remote = (count - 1) * CAP
+
+    def work(turn, carry):
+        slot = place_of(turn)
+        patch = patches.at[slot]
+        lane = lax.broadcasted_iota(jnp.int32, (PSF, 16, 128), 2)
+        taps = base[slot].astype(jnp.float32).reshape(PSF, 16, 128)
+        for step in range(B // 16):
+            first = 16 * step
+            turned = pltpu.roll(taps, first, 2) if first else taps
+            over = first + 56 - 128
+            if over > 0:
+                low = jnp.where(lane >= first, turned, 0.0)
+                high = jnp.where(lane < over, turned, 0.0)
+                tt[0:PSF, first : first + 16, 128:256] = high.astype(jnp.bfloat16)
+            else:
+                low = turned
+            tt[0:PSF, first : first + 16, 0:128] = low.astype(jnp.bfloat16)
+        total = None
+        for s in range(14, -1, -2):
+            acc = None
+            for q in range(3):
+                a = 16 * q + s
+                if a >= PSF:
+                    continue
+                band = tt[a : a + 2].reshape(256, 256)
+                term = lax.dot_general(patch[16 * q : 16 * q + 144, :], band,
+                                       (((1,), (1,)), ((), ())), preferred_element_type=jnp.float32)
+                acc = term if acc is None else acc + term
+            if total is None:
+                total = acc[:, 128:256]
+            else:
+                total = pltpu.roll(total, 143, 0) + acc[:, 128:256]
+            total = pltpu.roll(total, 143, 0) + acc[:, 0:128]
+        predicted = total[0:B]
+        residual = (keep[slot].astype(jnp.float32) * (predicted - observed[slot].astype(jnp.float32)))
+        residual = residual.astype(jnp.bfloat16)
+        residual_out[slot] = residual
+        wide = jnp.concatenate([residual.astype(jnp.float32), jnp.zeros((16, B), jnp.float32)], 0)
+        rbuf[32 : 32 + B, 0:128] = residual
+        rbuf[32 : 32 + B + 16, 128:256] = pltpu.roll(wide, 1, 0).astype(jnp.bfloat16)
+
+        back = None
+        for s in range(14, -1, -2):
+            acc = None
+            for q in range(3):
+                a = 16 * q + s
+                if a >= PSF:
+                    continue
+                band = tt[a : a + 2].reshape(256, 256)
+                term = jnp.dot(rbuf[32 - 16 * q : 32 - 16 * q + AROWS, :], band,
+                               preferred_element_type=jnp.float32)
+                acc = term if acc is None else acc + term
+            back = acc if back is None else pltpu.roll(back, 2, 0) + acc
+        tails = back[0:EXT, 128:256]
+        packed = tails[0:FOLD]
+        for third in range(1, 3):
+            packed = packed + pltpu.roll(tails[third * FOLD : (third + 1) * FOLD], 2 * HALO * third, 1)
+        outbox[slot] = jnp.concatenate([back[0:EXT, 0:128], packed], 0).astype(jnp.bfloat16)
+
+        @pl.when(turn < remote)
+        def _():
+            send(turn).start()
+
+        return carry
+
+    lax.fori_loop(0, count * CAP, work, 0)
+    for turn in range(CAP):
+        copies.append(pltpu.make_async_copy(
+            outbox.at[sky * CAP + turn], got.at[sky * CAP + turn], local_sem.at[turn]))
+        copies[-1].start()
+
+    def drain(turn, carry):
+        send(turn).wait()
+        return carry
+
+    lax.fori_loop(0, remote, drain, 0)
+    for copy in copies:
+        copy.wait()
+
+
+def run_pieces(asked, whole, base, observed, keep):
+    count = lax.axis_size("sky")
+    slots = count * CAP
+    vmem = pl.BlockSpec(memory_space=pltpu.VMEM)
+    hbm = pl.BlockSpec(memory_space=pl.ANY)
+    remote = (count - 1) * CAP
+    return pl.pallas_call(
+        functools.partial(piece_kernel, count),
+        out_shape=[
+            jax.ShapeDtypeStruct((slots, B, B), jnp.bfloat16),
+            jax.ShapeDtypeStruct((slots, PACKED, B), jnp.bfloat16),
+            jax.ShapeDtypeStruct(asked.shape, asked.dtype),
+        ],
+        in_specs=[hbm] + [vmem] * 4,
+        out_specs=[vmem, hbm, hbm],
+        scratch_shapes=[
+            pltpu.VMEM((slots, PACKED, B), jnp.bfloat16),
+            pltpu.VMEM((TAPS, B, 256), jnp.bfloat16),
+            pltpu.VMEM((32 + AROWS, 256), jnp.bfloat16),
+            pltpu.SemaphoreType.DMA((remote,)),
+            pltpu.SemaphoreType.DMA((remote,)),
+            pltpu.SemaphoreType.DMA((count - 1,)),
+            pltpu.SemaphoreType.DMA((count - 1,)),
+            pltpu.SemaphoreType.DMA((CAP + 1,)),
+        ],
+        compiler_params=pltpu.CompilerParams(
+            collective_id=1, has_side_effects=True, vmem_limit_bytes=48 * 2**20),
+        name="pieces",
+    )(asked, whole, base, observed, keep)
+
+
+def arrange_kernel(rows, cols, cells, order, whole, base, observed, keep,
+                   patch_out, base_out, observed_out, keep_out):
+    slot = pl.program_id(0)
+    row0 = pl.multiple_of(rows[slot], 128)
+    col0 = pl.multiple_of(cols[slot], 128)
+    window = whole[pl.ds(row0, 192), pl.ds(col0, 384)].astype(jnp.float32)
     shifted = window[ROWPAD - HALO : ROWPAD - HALO + AROWS]
     shifted = pltpu.roll(shifted, 384 - (COLPAD - HALO), 1)[:, 0:256]
-    patch[...] = shifted.astype(jnp.bfloat16)
-
-    total = None
-    for s in range(14, -1, -2):
-        acc = None
-        for q in range(3):
-            a = 16 * q + s
-            if a >= PSF:
-                continue
-            band = tt[a : a + 2].reshape(256, 256)
-            term = lax.dot_general(patch[16 * q : 16 * q + 144, :], band,
-                                   (((1,), (1,)), ((), ())), preferred_element_type=jnp.float32)
-            acc = term if acc is None else acc + term
-        if total is None:
-            total = acc[:, 128:256]
-        else:
-            total = pltpu.roll(total, 143, 0) + acc[:, 128:256]
-        total = pltpu.roll(total, 143, 0) + acc[:, 0:128]
-    predicted = total[0:B]
-    residual = (keep[0].astype(jnp.float32) * (predicted - observed[0].astype(jnp.float32)))
-    residual = residual.astype(jnp.bfloat16)
-    residual_out[0] = residual
-    wide = jnp.concatenate([residual.astype(jnp.float32), jnp.zeros((16, B), jnp.float32)], 0)
-    rbuf[32 : 32 + B, 0:128] = residual
-    rbuf[32 : 32 + B + 16, 128:256] = pltpu.roll(wide, 1, 0).astype(jnp.bfloat16)
-
-    back = None
-    for s in range(14, -1, -2):
-        acc = None
-        for q in range(3):
-            a = 16 * q + s
-            if a >= PSF:
-                continue
-            band = tt[a : a + 2].reshape(256, 256)
-            term = jnp.dot(rbuf[32 - 16 * q : 32 - 16 * q + AROWS, :], band,
-                           preferred_element_type=jnp.float32)
-            acc = term if acc is None else acc + term
-        back = acc if back is None else pltpu.roll(back, 2, 0) + acc
-    tails = back[0:EXT, 128:256]
-    packed = tails[0:FOLD]
-    for third in range(1, 3):
-        packed = packed + pltpu.roll(tails[third * FOLD : (third + 1) * FOLD], 2 * HALO * third, 1)
-    adjoint_out[0] = jnp.concatenate([back[0:EXT, 0:128], packed], 0).astype(jnp.bfloat16)
-
-
-def run_pieces(rows, cols, cells, slots, whole, base, observed, keep, slot_total):
-    count = observed.shape[0]
-    flops = count * 21 * 2 * 256 * 256 * (144 + AROWS)
+    patch_out[0] = shifted.astype(jnp.bfloat16)
+    base_out[...] = base[...]
+    observed_out[...] = observed[...]
+    keep_out[...] = keep[...].astype(jnp.float32).astype(jnp.bfloat16)
+
+
+def arrange(rows, cols, cells, order, whole, base, observed, keep):
+    slots = rows.shape[0]
+    shapes = [(AROWS, 256), (PSF * 16, 128), (B, B), (B, B)]
+
+    def by_order(i, r, c, k, o):
+        return (o[i], 0, 0)
+
     return pl.pallas_call(
-        piece_kernel,
+        arrange_kernel,
         grid_spec=pltpu.PrefetchScalarGridSpec(
             num_scalar_prefetch=4,
-            grid=(count,),
+            grid=(slots,),
             in_specs=[
-                pl.BlockSpec(memory_space=pl.ANY),
-                pl.BlockSpec((1, PSF + 1, B, 256), lambda p, r, c, k, s: (k[p], 0, 0, 0)),
-                pl.BlockSpec((1, B, B), lambda p, r, c, k, s: (p, 0, 0)),
-                pl.BlockSpec((1, B, B), lambda p, r, c, k, s: (p, 0, 0)),
+                pl.BlockSpec(whole.shape, lambda i, r, c, k, o: (0, 0)),
+                pl.BlockSpec((1, PSF * 16, 128), lambda i, r, c, k, o: (k[i], 0, 0)),
+                pl.BlockSpec((1, B, B), by_order),
+                pl.BlockSpec((1, B, B), by_order),
             ],
-            out_specs=[
-                pl.BlockSpec((1, B, B), lambda p, r, c, k, s: (p, 0, 0)),
-                pl.BlockSpec((1, PACKED, B), lambda p, r, c, k, s: (s[p], 0, 0)),
-            ],
-            scratch_shapes=[
-                pltpu.VMEM((2, 192, 384), jnp.bfloat16),
-                pltpu.VMEM((AROWS, 256), jnp.bfloat16),
-                pltpu.VMEM((32 + AROWS, 256), jnp.bfloat16),
-                pltpu.SemaphoreType.DMA((2,)),
-            ],
+            out_specs=[pl.BlockSpec((1,) + s, lambda i, r, c, k, o: (i, 0, 0)) for s in shapes],
         ),
-        out_shape=[
-            jax.ShapeDtypeStruct((count, B, B), jnp.bfloat16),
-            jax.ShapeDtypeStruct((slot_total, PACKED, B), jnp.bfloat16),
-        ],
-        compiler_params=pltpu.CompilerParams(vmem_limit_bytes=56 * 2**20),
-        cost_estimate=pl.CostEstimate(flops=flops, bytes_accessed=16 * 2**20, transcendentals=0),
-        name="pieces",
-    )(rows, cols, cells, slots, whole, base, observed, keep)
+        out_shape=[jax.ShapeDtypeStruct((slots,) + s, jnp.bfloat16) for s in shapes],
+        compiler_params=pltpu.CompilerParams(vmem_limit_bytes=40 * 2**20),
+        name="arrange",
+    )(rows, cols, cells, order, whole, base, observed, keep)
 
 
 def shards(sky_model, exposure_data, pixel_mask, block_owner, block_local, psf_cell, psf_table):
@@ -514,12 +554,18 @@
     whole, table = gather_model(sky_model, kernels)
     row_start = (owner_sky * block_rows + block_local // per_row) * B
     col_start = block_local % per_row * B
-    residuals, adjoints = run_pieces(
-        row_start, col_start, psf_cell, slot_index, whole, table, exposure_data, pixel_mask, slot_total
+    order = jnp.sum(jnp.where(named, jnp.arange(piece_count, dtype=jnp.int32)[None, :], 0), axis=1)
+
+    def by_slot(values):
+        return jnp.sum(jnp.where(named, values[None, :], 0), axis=1)
+
+    arranged = arrange(
+        by_slot(row_start), by_slot(col_start), by_slot(psf_cell), order, whole, table,
+        exposure_data, pixel_mask,
     )
-    received, asked = exchange(adjoints.reshape(sky_count, CAP, PACKED, B), requests)
+    residuals, received, asked = run_pieces(requests, *arranged)
     ids = asked[:, 0, :CAP].reshape(slot_total)
-    parts = fold(ids, received.reshape(slot_total, PACKED, B), stripe_rows, stripe_cols, exp_count)
+    parts, residuals = fold(ids, slot_index, received, residuals, stripe_rows, stripe_cols, exp_count)
     return (reduce_parts(parts), residuals)
 
 

time: 117 us -> 104 us (0.89)
  Pallas kernels: 107 us -> 91.6 us
  local copies, waits for them, and re-layouts: 6.57 us -> 8.64 us
    pallas_call x2, Pallas kernels: 50 us -> 38.3 us  [the longest x1 33.2 us: run_pieces(): pl.pallas_call(functools.partial(piece_kernel, count), out_shape=[jax.Sha...]
    pallas_call x1, Pallas kernels: 20.7 us -> 14.1 us  [reduce_parts(): pl.pallas_call(functools.partial(reduce_kernel, skies, exps), out_shape=j...]
    pallas_call x1, Pallas kernels: 33.8 us -> 36.2 us  [gather_model(): pl.pallas_call(functools.partial(gather_kernel, count, cuts), out_shape=[...]
    unnamed x9 -> x13, local copies, waits for them, and re-layouts: 5.28 us -> 7.35 us
where the time goes in v4:
time: 104 us; the launch traced here: 103 us
  Pallas kernels  91.6 us (88%)
  local copies, waits for them, and re-layouts  8.64 us (8%)
  other arithmetic  2.44 us (2%)
    pallas_call x1, Pallas kernels, gather_model(): pl.pallas_call(functools.partial(gather_kernel, count, cuts), out_shape=[...  36.2 us
    pallas_call x1, Pallas kernels, run_pieces(): pl.pallas_call(functools.partial(piece_kernel, count), out_shape=[jax.Sha...  33.2 us
    pallas_call x1, Pallas kernels, reduce_parts(): pl.pallas_call(functools.partial(reduce_kernel, skies, exps), out_shape=j...  14.1 us
    unnamed x13, local copies, waits for them, and re-layouts  7.35 us
    pallas_call x1, Pallas kernels, arrange(): pl.pallas_call(arrange_kernel, grid_spec=pltpu.PrefetchScalarGridSpec(num...  5.07 us
    pallas_call x1, Pallas kernels, fold(): pl.pallas_call(functools.partial(fold_kernel, stripe_rows, stripe_cols, e...  2.96 us

profile of v4, /device:TPU:1, one launch (start us, length us, event | category | flops | bytes accessed | tf_op | source)
XLA Modules:
  0.0 103.4 jit_solution(8200165798020830433)
XLA Ops:
  0.6 0.9 convert_reduce_fusion
  1.5 0.7 broadcast_add_fusion.1
  2.2 0.8 select_reduce_fusion
  3.1 1.1 %reshape.34 = bf16[16,41,41]{2,1,0:T(8,128)(2,1)S(1)} reshape(bf16[16,1681]{1,0:T(8,128)(2,1)} %param.13) | data formatting | bytes 107584 | tf_op jit(solution)/shard_map/reshape | solution.py:551
  4.2 0.0 copy-start.2
  4.2 1.0 copy-done.2
  5.2 36.2 %gather_model.1 = (bf16[2112,1280]{1,0:T(8,128)(2,1)}, bf16[16,656,128]{2,1,0:T(8,128)(2,1)S(1)}) custom-call(bf16[256,1024]{1,0:T(8,128)(2,1)S(1)} %copy-done.2, bf16[16,48,128]{2,1,0:T(8,128)(2,1)S(1)} %pad.9.kernels), custom_call_target="tpu_custom_call" | custom-call | tf_op jit(solution)/shard_map/gather_model/pallas_call | solution.py:186
  41.4 0.0 copy-start.1
  41.4 1.2 %copy-done.1 = s32[16,128,128]{2,1,0:T(8,128)S(1)} copy-done((s32[16,128,128]{2,1,0:T(8,128)S(1)}, s32[16,128,128]{2,1,0:T(8,128)}, u32[]{:S(2)}) %copy-start.1) | copy-done | bytes 1048600
  42.7 0.0 copy-start.5
  42.7 1.0 %copy-done.5 = bf16[16,128,128]{2,1,0:T(8,128)(2,1)S(1)} copy-done((bf16[16,128,128]{2,1,0:T(8,128)(2,1)S(1)}, bf16[16,128,128]{2,1,0:T(8,128)(2,1)}, u32[]{:S(2)}) %copy-start.5) | copy-done | bytes 524312
  43.7 5.1 %arrange.1 = (bf16[16,176,256]{2,1,0:T(8,128)(2,1)S(1)}, bf16[16,656,128]{2,1,0:T(8,128)(2,1)S(1)}, bf16[16,128,128]{2,1,0:T(8,128)(2,1)S(1)}, bf16[16,128,128]{2,1,0:T(8,128)(2,1)S(1)}) custom-call(s32[16]{0:T(128)S(1)} %get-tuple-element.27.rows, s32[16]{0:T(128)S(1)} %get-tuple-element.26.cols, s32[16]{0:T(128)S(1)} %get-tuple-element.25.cells, ...), custom_call_target="tpu_custom_call" | custom-call | tf_op jit(solution)/shard_map/arrange/pallas_call | solution.py:513
  48.8 0.0 copy-start
  48.8 1.5 %copy-done = bf16[16,656,128]{2,1,0:T(8,128)(2,1)} copy-done((bf16[16,656,128]{2,1,0:T(8,128)(2,1)}, bf16[16,656,128]{2,1,0:T(8,128)(2,1)S(1)}, u32[]{:S(2)}) %copy-start) | copy-done | bytes 2687000
  50.3 0.1 sub.10
  50.4 33.2 %pieces.1 = (bf16[16,128,128]{2,1,0:T(8,128)(2,1)S(1)}, bf16[16,224,128]{2,1,0:T(8,128)(2,1)S(1)}, s32[8,8,128]{2,1,0:T(8,128)S(1)}) custom-call(s32[8,8,128]{2,1,0:T(8,128)S(1)} %pad.8.asked, bf16[16,176,256]{2,1,0:T(8,128)(2,1)S(1)} %get-tuple-element.15.patches, bf16[16,656,128]{2,1,0:T(8,128)(2,1)} %copy-done, ...), custom_call_target="tpu_custom_call" | custom-call | tf_op jit(solution)/shard_map/pieces/pallas_call | solution.py:467
  83.6 0.0 copy-start.3
  83.6 0.8 copy-done.3
  84.4 0.1 reshape_squeeze.3.ids
  84.5 0.0 copy-start.4
  84.5 1.0 %copy-done.4 = bf16[16,128,128]{2,1,0:T(8,128)(2,1)S(1)} copy-done((bf16[16,128,128]{2,1,0:T(8,128)(2,1)S(1)}, bf16[16,128,128]{2,1,0:T(8,128)(2,1)}, u32[]{:S(2)}) %copy-start.4) | copy-done | bytes 524312
  85.6 3.0 %fold.1 = (bf16[4,320,256]{2,1,0:T(8,128)(2,1)S(1)}, bf16[16,128,128]{2,1,0:T(8,128)(2,1)}) custom-call(s32[16]{0:T(128)S(1)} %reshape_squeeze.3.ids, s32[16]{0:T(128)S(1)} %get-tuple-element.32.slots, bf16[16,224,128]{2,1,0:T(8,128)(2,1)S(1)} %get-tuple-element.20.parts, bf16[16,128,128]{2,1,0:T(8,128)(2,1)S(1)} %copy-done.4), custom_call_target="tpu_custom_call" | custom-call | tf_op jit(solution)/shard_map/fold/pallas_call | solution.py:251
  88.5 14.1 %reduce_parts.1 = f32[256,256]{1,0:T(8,128)S(1)} custom-call(bf16[4,320,256]{2,1,0:T(8,128)(2,1)S(1)} %get-tuple-element.22.parts), custom_call_target="tpu_custom_call" | custom-call | tf_op jit(solution)/shard_map/reduce_parts/pallas_call | solution.py:329
  102.7 0.7 copy.13
  (4 shorter events, 0.1 us)
Async XLA Ops:
  4.2 1.0 %copy-start.2 = (bf16[256,1024]{1,0:T(8,128)(2,1)S(1)}, bf16[256,1024]{1,0:T(8,128)(2,1)}, u32[]{:S(2)}) copy-start(bf16[256,1024]{1,0:T(8,128)(2,1)} %stripe.1) | copy-start | bytes 1572868
  41.4 1.2 %copy-start.1 = (s32[16,128,128]{2,1,0:T(8,128)S(1)}, s32[16,128,128]{2,1,0:T(8,128)}, u32[]{:S(2)}) copy-start(s32[16,128,128]{2,1,0:T(8,128)} %keep.1) | copy-start | bytes 3145732
  42.7 1.0 %copy-start.5 = (bf16[16,128,128]{2,1,0:T(8,128)(2,1)S(1)}, bf16[16,128,128]{2,1,0:T(8,128)(2,1)}, u32[]{:S(2)}) copy-start(bf16[16,128,128]{2,1,0:T(8,128)(2,1)} %observed.1) | copy-start | bytes 1572868
  48.8 1.5 %copy-start = (bf16[16,656,128]{2,1,0:T(8,128)(2,1)}, bf16[16,656,128]{2,1,0:T(8,128)(2,1)S(1)}, u32[]{:S(2)}) copy-start(bf16[16,656,128]{2,1,0:T(8,128)(2,1)S(1)} %get-tuple-element.16.base) | copy-start | bytes 8060932
  83.6 0.8 copy-start.3
  84.5 1.0 %copy-start.4 = (bf16[16,128,128]{2,1,0:T(8,128)(2,1)S(1)}, bf16[16,128,128]{2,1,0:T(8,128)(2,1)}, u32[]{:S(2)}) copy-start(bf16[16,128,128]{2,1,0:T(8,128)(2,1)} %copy-done.3) | copy-start | bytes 1572868
